TPU v7x, 32 devices: a whole 2x2x4 slice. The times are simulated.
32 devices in a mesh: groups: 2 (over x), seq: 16 (over z, y, core).
Axes of the slice: x: 2, y: 2, z: 4, core: 2. Of those that a mesh axis runs over, the one named last changes fastest.
Arguments:
- patches: bfloat16 [4096, 1176], P(('groups', 'seq')), parts along dimension 0, may hold values from -6 to 6
- row_owner: int32 [4096, 1], P(('groups', 'seq')), parts along dimension 0, may hold values from 0 to 15; in each aligned block of 128 rows (0 to 127, 128 to 255, ...) at most 16 rows name the same one
- window_slot: int32 [4096], P(('groups', 'seq')), parts along dimension 0, may hold values from 0 to 3
- w_patch: bfloat16 [1176, 1280], replicated, may hold values from -1 to 1
- vit_gain: float32 [1280], replicated, may hold values from 0.1 to 1.9
- w_qkv: bfloat16 [1280, 1920], replicated, may hold values from -1 to 1
- queries: bfloat16 [4096, 4096], P(('groups', 'seq')), parts along dimension 0, may hold values from -36 to 36
- new_kv: bfloat16 [4096, 1024], P(('groups', 'seq')), parts along dimension 0, may hold values from -6 to 6
- kv_cache: bfloat16 [2048, 16, 1024], P(('groups', 'seq')), parts along dimension 0, may hold values from -6 to 6
- block_table: int32 [32, 64], P(('groups', 'seq')), parts along dimension 0, may hold values from -1 to 1023, as said below
Outputs:
- vision_out: bfloat16 [4096, 640], P(('groups', 'seq')), parts along dimension 0
- attention_out: bfloat16 [4096, 4096], P(('groups', 'seq')), parts along dimension 0
There are 2 independent parts, one for each index of `groups`. A program takes and returns all parts, laid end to end along the dimension named above; an argument that names none is the same for every part. Nothing has to cross between parts.
Inputs may be any that keep to these rules, and one draw needn't show every extreme that they name: `row_owner`: in the rows of one device, each owner is named by at most 16 rows. `block_table`: block b is stored on device b // 64. Each row lists 8 or more distinct blocks, then -1 entries; at most 8 of a row's blocks lie on one device.
All inputs are finite; a program needn't handle non-finite values.
Results may differ from a plain program's by a relative error of at most 0.0093.
Values may be sent and summed in bfloat16 or wider, within the bound.
No kernel may reach another device: no remote copies, remote signals or barrier semaphores. Data moves between devices by JAX's collectives and lax.ppermute only.
A program may use at most 64 MiB of HBM per device.

v0:
```python
import functools

import jax
import jax.numpy as jnp
from jax import lax
from jax.experimental import pallas as pl
from jax.experimental.pallas import tpu as pltpu
from jax.sharding import PartitionSpec as P

VHEADS = 8
VHD = 80
QHEADS = 32
KVH = 4
HD = 128
LANES = 128
CHUNK_BLOCKS = 16
HEADS_TILE = 2
LOG2E = 1.4426950408889634
HIDDEN = -1e30
VMEM_BYTES = 56 * 1024 * 1024
ROOM_STEP = 8
EARLY_STEPS = (4, 5, 2, 3)


def iota(shape, axis):
    return lax.broadcasted_iota(jnp.int32, shape, axis)


def count(hits, axis):
    return jnp.sum(hits.astype(jnp.float32), axis=axis, keepdims=True).astype(jnp.int32)


def as_row(column):
    size = column.shape[0]
    diagonal = iota((size, size), 0) == iota((size, size), 1)
    return jnp.sum(jnp.where(diagonal, column, 0).astype(jnp.float32), axis=0, keepdims=True).astype(jnp.int32)


def as_column(row):
    size = row.shape[1]
    diagonal = iota((size, size), 0) == iota((size, size), 1)
    return jnp.sum(jnp.where(diagonal, row, 0).astype(jnp.float32), axis=1, keepdims=True).astype(jnp.int32)


def embed_kernel(
    capacity,
    per_owner,
    blocks_dev,
    lanes,
    patches_ref,
    w_ref,
    gain_ref,
    owner_ref,
    window_ref,
    table_ref,
    payload_ref,
    target_ref,
    request_ref,
    live_ref,
    turned_ref,
    embedded_ref,
):
    step = pl.program_id(0)
    width = w_ref.shape[1]

    @pl.when(step == 0)
    def _():
        turned_ref[...] = patches_ref[...].T

    piece = jnp.dot(turned_ref[...], w_ref[...], preferred_element_type=jnp.float32)
    embedded_ref[:, pl.ds(pl.multiple_of(step * width, width), width)] = piece.astype(jnp.bfloat16)

    @pl.when(step == pl.num_programs(0) - 1)
    def _():
        slots = payload_ref.shape[0]
        vit = embedded_ref.shape[1]
        rows = owner_ref.shape[1]
        owner_row = owner_ref[...]
        owner_column = as_column(owner_row)
        same = owner_column == owner_row
        first, second = iota((rows, rows), 0), iota((rows, rows), 1)
        rank_row = count(same & (first < second), 0)
        rank_column = count(same & (second < first), 1)
        target_ref[...] = owner_column * capacity + rank_column
        placed = (owner_row * capacity + rank_row) == iota((slots, rows), 0)
        windows = (
            jnp.sum(jnp.where(placed, window_ref[...] + 1, 0).astype(jnp.float32), axis=1, keepdims=True)
            - 1.0
        )
        note_list(capacity, per_owner, blocks_dev, lanes, windows, table_ref, payload_ref.at[:, vit:], request_ref, live_ref)

        widened = embedded_ref[...].astype(jnp.float32)
        factor = lax.rsqrt(jnp.mean(widened * widened, axis=1, keepdims=True) + 1e-06)
        normed = (widened * factor * gain_ref[...].reshape(1, -1)).astype(jnp.bfloat16)
        payload_ref[:, :vit] = jnp.dot(
            placed.astype(jnp.bfloat16), normed, preferred_element_type=jnp.float32
        ).astype(jnp.bfloat16)


def note_list(capacity, per_owner, blocks_dev, lanes, windows, table_ref, notes_ref, request_ref, live_ref):
    slots = notes_ref.shape[0]
    table_row = table_ref[...]
    entries = table_row.shape[1]
    live_row = table_row >= 0
    holder_row = jnp.where(live_row, table_row // blocks_dev, -1)
    local_row = jnp.where(live_row, table_row % blocks_dev, 0)
    lane = iota((slots, LANES), 1)
    before = iota((entries, entries), 0) < iota((entries, entries), 1)
    if lanes is None:
        holder_rank = count((as_column(holder_row) == holder_row) & before, 0)
        request_row = jnp.where(live_row, holder_row * per_owner + holder_rank, -1)
        first_request = jnp.sum(
            jnp.where(iota((1, entries), 1) == 0, request_row, 0).astype(jnp.float32), axis=1, keepdims=True
        ).astype(jnp.int32)
        request_ref[...] = jnp.where(live_row, request_row, first_request)
        live_ref[...] = jnp.broadcast_to(count(live_row, 1), live_ref.shape)
        placed_row = jnp.where(live_row, holder_row * capacity + holder_rank, -1)
        asked = jnp.sum(
            jnp.where(placed_row == iota((slots, entries), 0), local_row + 1, 0).astype(jnp.float32),
            axis=1,
            keepdims=True,
        )
        notes = jnp.where(lane == 0, windows, jnp.where(lane == 1, asked - 1.0, 0.0))
        notes_ref[...] = notes.astype(jnp.bfloat16)
        return
    regions = slots // capacity // lanes
    after = iota((entries, entries), 1) < iota((entries, entries), 0)
    region_row = jnp.where(live_row, holder_row // lanes, -1)
    region_column = as_column(region_row)
    region_rank = count((region_column == region_row) & after, 1)
    local_column, member_column = as_column(local_row), as_column(jnp.where(live_row, holder_row % lanes, 0))
    place = iota((slots, LANES), 0)
    slot_row, slot_region = place % capacity, place // (capacity * lanes)
    pad = jnp.zeros((1, LANES - entries), jnp.float32)
    notes = jnp.where(lane == entries, windows, 0.0)
    most = jnp.zeros((1, 1), jnp.int32)
    live_ref[...] = jnp.zeros(live_ref.shape, jnp.int32)
    for region in range(regions):
        listed = (region_column == region) & (region_rank == iota((entries, entries), 1))
        pick = lambda column: jnp.sum(
            jnp.where(listed, column, 0).astype(jnp.float32), axis=0, keepdims=True
        )
        amount = count(region_row == region, 1)
        most = jnp.maximum(most, amount)
        live_ref[:, region : region + 1] = amount
        locals_row = jnp.concatenate([pick(local_column + 1) - 1.0, pad], axis=1)
        members_row = jnp.concatenate([pick(member_column), pad], axis=1)
        here = (slot_region == region) & (lane < entries)
        notes = jnp.where(here & (slot_row == 0), locals_row, notes)
        notes = jnp.where(here & (slot_row == 1), members_row, notes)
    notes = jnp.where(lane == entries + 1, most.astype(jnp.float32), notes)
    notes_ref[...] = notes.astype(jnp.bfloat16)
    request_ref[...] = jnp.zeros(request_ref.shape, jnp.int32)


def embed_and_route(
    patches, w_patch, vit_gain, row_owner, window_slot, block_table, capacity, slots, per_owner, blocks_dev, lanes
):
    rows, patch = patches.shape
    vit = w_patch.shape[1]
    entries = block_table.shape[1]
    width = vit // 2
    whole = lambda *shape: pl.BlockSpec(shape, lambda step: (0,) * len(shape))
    return pl.pallas_call(
        functools.partial(embed_kernel, capacity, per_owner, blocks_dev, lanes),
        grid=(vit // width,),
        out_shape=(
            jax.ShapeDtypeStruct((slots, vit + LANES), jnp.bfloat16),
            jax.ShapeDtypeStruct((rows, 1), jnp.int32),
            jax.ShapeDtypeStruct((1, entries), jnp.int32),
            jax.ShapeDtypeStruct((1, LANES), jnp.int32),
        ),
        in_specs=[
            whole(patch, rows),
            pl.BlockSpec((patch, width), lambda step: (0, step)),
            whole(vit),
            whole(1, rows),
            whole(1, rows),
            whole(1, entries),
        ],
        out_specs=(whole(slots, vit + LANES), whole(rows, 1), whole(1, entries), whole(1, LANES)),
        scratch_shapes=[pltpu.VMEM((rows, patch), jnp.bfloat16), pltpu.VMEM((rows, vit), jnp.bfloat16)],
        compiler_params=pltpu.CompilerParams(vmem_limit_bytes=VMEM_BYTES),
        cost_estimate=pl.CostEstimate(
            flops=2 * rows * patch * vit + 2 * slots * rows * vit,
            bytes_accessed=2 * patch * vit + 2 * rows * patch + 2 * slots * vit,
            transcendentals=rows,
        ),
        name="embed_and_route",
    )(
        patches.T, w_patch, vit_gain, row_owner.reshape(1, rows),
        window_slot.reshape(1, rows), block_table,
    )


def prompt_groups(query_ref, tile):
    tokens = query_ref.shape[0]
    group_size = QHEADS // KVH
    tile_rows = HEADS_TILE * tokens

    def group_step(group, carry):
        for part in range(group_size // HEADS_TILE):
            head = group * group_size + part * HEADS_TILE
            queries = jnp.concatenate(
                [
                    query_ref[:, pl.ds(pl.multiple_of((head + i) * HD, HD), HD)]
                    for i in range(HEADS_TILE)
                ],
                axis=0,
            )
            tile(group, queries, pl.ds(pl.multiple_of(head * tokens, tile_rows), tile_rows))
        return carry

    lax.fori_loop(0, KVH, group_step, 0)


def prompt_scores(queries, keys):
    return lax.dot_general(
        queries, keys, (((1,), (1,)), ((), ())), preferred_element_type=jnp.float32
    ) * (HD ** (-0.5) * LOG2E)


def with_ones(values):
    return jnp.concatenate([values, jnp.ones_like(values)], axis=1)


def head_columns(head):
    return pl.ds(pl.multiple_of(head * HD, HD), HD)


def prompt_begin(query_ref, fresh_ref, top_ref, sum_ref):
    tokens = query_ref.shape[0]
    causal = iota((tokens, tokens), 1) <= iota((tokens, tokens), 0)
    causal = jnp.concatenate([causal.astype(jnp.int32)] * HEADS_TILE, axis=0) > 0

    def tile(group, queries, rows):
        keys, values = fresh_ref[:, head_columns(group)], fresh_ref[:, head_columns(KVH + group)]
        scores = jnp.where(causal, prompt_scores(queries, keys), HIDDEN)
        top = jnp.max(scores, axis=1, keepdims=True)
        weights = jnp.exp2(scores - top).astype(jnp.bfloat16)
        top_ref[rows, :] = jnp.broadcast_to(top, (scores.shape[0], HD))
        sum_ref[rows, :] = jnp.dot(weights, with_ones(values), preferred_element_type=jnp.float32)

    prompt_groups(query_ref, tile)


def prompt_add(query_ref, top_ref, sum_ref, take, shown):
    chunk_keys = shown.shape[1]

    def tile(group, queries, rows):
        scores = jnp.where(shown, prompt_scores(queries, take(group)), HIDDEN)
        old_top = top_ref[rows, :]
        top = jnp.maximum(old_top, jnp.max(scores, axis=1, keepdims=True))
        shrink = jnp.exp2(old_top - top)
        weights = jnp.exp2(scores - jnp.concatenate([top] * (chunk_keys // HD), axis=1))
        top_ref[rows, :] = top
        sum_ref[rows, :] = sum_ref[rows, :] * jnp.concatenate([shrink, shrink], axis=1) + jnp.dot(
            weights.astype(jnp.bfloat16), with_ones(take(KVH + group)), preferred_element_type=jnp.float32
        )

    prompt_groups(query_ref, tile)


def prompt_end(out_ref, sum_ref):
    tokens = out_ref.shape[0]

    def finish(head, carry):
        blended = sum_ref[pl.ds(pl.multiple_of(head * tokens, tokens), tokens), :]
        out_ref[:, head_columns(head)] = (blended[:, :HD] / blended[:, HD:]).astype(jnp.bfloat16)
        return carry

    lax.fori_loop(0, QHEADS, finish, 0)


def listed_prompt_kernel(
    request_ref, live_ref, query_ref, fresh_ref, blocks_ref, out_ref, top_ref, sum_ref, kv_ref, sems
):
    block_tokens = kv_ref.shape[1]
    chunk_keys = CHUNK_BLOCKS * block_tokens
    live_blocks = live_ref[0, 0]
    chunks = (live_blocks + (CHUNK_BLOCKS - 1)) // CHUNK_BLOCKS

    def fetch(chunk, carry):
        def one(place, inner):
            entry = chunk * CHUNK_BLOCKS + place
            pltpu.make_async_copy(
                blocks_ref.at[request_ref[0, entry]], kv_ref.at[entry], sems.at[chunk]
            ).start()
            return inner

        return lax.fori_loop(0, CHUNK_BLOCKS, one, carry)

    lax.fori_loop(0, chunks, fetch, 0)
    prompt_begin(query_ref, fresh_ref, top_ref, sum_ref)

    def visit(chunk, carry):
        first = chunk * CHUNK_BLOCKS
        pltpu.make_async_copy(
            blocks_ref.at[pl.ds(0, CHUNK_BLOCKS)], kv_ref.at[pl.ds(first, CHUNK_BLOCKS)], sems.at[chunk]
        ).wait()
        shown = iota((1, chunk_keys), 1) < (live_blocks - first) * block_tokens
        take = lambda head: kv_ref[pl.ds(first, CHUNK_BLOCKS), :, head_columns(head)].reshape(chunk_keys, HD)
        prompt_add(query_ref, top_ref, sum_ref, take, shown)
        return carry

    lax.fori_loop(0, chunks, visit, 0)
    prompt_end(out_ref, sum_ref)


def striped_prompt_kernel(
    lanes, live_ref, query_ref, fresh_ref, target_ref, striped_ref, out_ref, vision_ref, top_ref, sum_ref
):
    extra = vision_ref.shape[1] // LANES
    regions, room, block_tokens = striped_ref.shape[0] // lanes, striped_ref.shape[1] - extra, striped_ref.shape[2]
    chunk_keys = CHUNK_BLOCKS * block_tokens
    prompt_begin(query_ref, fresh_ref, top_ref, sum_ref)
    chunks = [(live_ref[0, region] + (CHUNK_BLOCKS - 1)) // CHUNK_BLOCKS for region in range(regions)]

    def visit(turn, carry):
        region = (turn >= chunks[0]).astype(jnp.int32)
        chunk = turn - region * chunks[0]
        first = jnp.minimum(chunk * CHUNK_BLOCKS, room - CHUNK_BLOCKS)
        key = iota((1, chunk_keys), 1)
        shown = (key < (live_ref[0, region] - first) * block_tokens) & (
            key >= (chunk * CHUNK_BLOCKS - first) * block_tokens
        )
        take = lambda lane: striped_ref[region * lanes + lane, pl.ds(first, CHUNK_BLOCKS)].reshape(chunk_keys, HD)
        prompt_add(query_ref, top_ref, sum_ref, take, shown)
        return carry

    lax.fori_loop(0, chunks[0] + chunks[1], visit, 0)
    prompt_end(out_ref, sum_ref)
    rows, slots = target_ref.shape[0], striped_ref.shape[0] * block_tokens
    picked = (target_ref[...] == iota((rows, slots), 1)).astype(jnp.bfloat16)
    for tile in range(extra):
        vision_ref[:, tile * LANES : (tile + 1) * LANES] = jnp.dot(
            picked, striped_ref[:, room + tile].reshape(slots, LANES), preferred_element_type=jnp.float32
        ).astype(jnp.bfloat16)


def prompt_attention(kernel, scalars, operands, specs, outs, scratch, keys, name):
    tokens, width = operands[0].shape
    kv_width = operands[1].shape[1]
    whole = lambda shape: pl.BlockSpec(shape, lambda *_: (0,) * len(shape))
    outs = [(tokens, width)] + outs
    return pl.pallas_call(
        kernel,
        out_shape=tuple(jax.ShapeDtypeStruct(shape, jnp.bfloat16) for shape in outs),
        grid_spec=pltpu.PrefetchScalarGridSpec(
            num_scalar_prefetch=len(scalars),
            grid=(1,),
            in_specs=[spec or whole(operand.shape) for operand, spec in zip(operands, specs)],
            out_specs=tuple(whole(shape) for shape in outs),
            scratch_shapes=[
                pltpu.VMEM((QHEADS * tokens, HD), jnp.float32),
                pltpu.VMEM((QHEADS * tokens, 2 * HD), jnp.float32),
            ]
            + scratch,
        ),
        compiler_params=pltpu.CompilerParams(vmem_limit_bytes=VMEM_BYTES),
        cost_estimate=pl.CostEstimate(
            flops=4 * tokens * keys * width,
            bytes_accessed=4 * tokens * width + 2 * keys * kv_width,
            transcendentals=tokens * QHEADS * keys,
        ),
        name=name,
    )(*scalars, *operands)


def listed_prompt(request, live, queries, new_kv, blocks):
    entries, block_tokens = request.shape[1], blocks.shape[1]
    chunks = -(-entries // CHUNK_BLOCKS)
    scratch = [
        pltpu.VMEM((chunks * CHUNK_BLOCKS, block_tokens, new_kv.shape[1]), jnp.bfloat16),
        pltpu.SemaphoreType.DMA((chunks,)),
    ]
    return prompt_attention(
        listed_prompt_kernel, (request, live), (queries, new_kv, blocks),
        (None, None, pl.BlockSpec(memory_space=pl.ANY)), [], scratch,
        entries * block_tokens + queries.shape[0], "listed_prompt",
    )[0]


def striped_prompt(lanes, extra, live, queries, new_kv, target, striped):
    keys = striped.shape[1] * striped.shape[2] + queries.shape[0]
    return prompt_attention(
        functools.partial(striped_prompt_kernel, lanes), (live,), (queries, new_kv, target, striped),
        (None,) * 4, [(target.shape[0], extra * LANES)], [], keys, "striped_prompt",
    )


def stripe_kernel(lanes, steps, cache_ref, *refs):
    out_refs, held_ref, in_sems, out_sems = refs[:-3], refs[-3], refs[-2], refs[-1]
    member = lax.axis_index("seq") % lanes
    chunks = in_sems.shape[0]
    size = cache_ref.shape[0] // chunks
    taken, given = [], []
    for chunk in range(chunks):
        part = pl.ds(chunk * size, size)
        taken.append(pltpu.make_async_copy(cache_ref.at[part], held_ref.at[part], in_sems.at[chunk]))
        taken[-1].start()
    for chunk in range(chunks):
        part = pl.ds(chunk * size, size)
        taken[chunk].wait()
        for place, step in enumerate(steps):
            column = pl.multiple_of((member ^ step) * LANES, LANES)
            given.append(
                pltpu.make_async_copy(
                    held_ref.at[part, :, pl.ds(column, LANES)],
                    out_refs[place].at[part],
                    out_sems.at[chunk, place],
                )
            )
            given[-1].start()
    for copy in given:
        copy.wait()


def stripe(lanes, steps, kv_cache):
    blocks, block_tokens, _ = kv_cache.shape
    chunks = 4
    piece = jax.ShapeDtypeStruct((blocks, block_tokens, LANES), jnp.bfloat16)
    return pl.pallas_call(
        functools.partial(stripe_kernel, lanes, steps),
        out_shape=(piece,) * len(steps),
        in_specs=[pl.BlockSpec(memory_space=pl.ANY)],
        out_specs=(pl.BlockSpec(memory_space=pl.ANY),) * len(steps),
        scratch_shapes=[
            pltpu.VMEM(kv_cache.shape, jnp.bfloat16),
            pltpu.SemaphoreType.DMA((chunks,)),
            pltpu.SemaphoreType.DMA((chunks, len(steps))),
        ],
        compiler_params=pltpu.CompilerParams(vmem_limit_bytes=VMEM_BYTES),
        name="stripe",
    )(kv_cache)


def gather_kernel(lanes, steps, entries, notes_ref, attended_ref, *refs):
    piece_refs = refs[:lanes]
    out_ref, held_ref, ready_ref, wide_ref, index_ref, scalar_ref, sems, out_sems = refs[lanes:]
    blocks = piece_refs[0].shape[0]
    readers, extra = attended_ref.shape[0], attended_ref.shape[1]
    room = out_ref.shape[1] - extra
    capacity = notes_ref.shape[0] // readers
    copies = [
        pltpu.make_async_copy(piece_ref, held_ref.at[pl.ds(step * blocks, blocks)], sems.at[step])
        for step, piece_ref in zip(steps, piece_refs)
    ]
    for copy in copies:
        copy.start()

    wide_ref[...] = notes_ref[...].astype(jnp.float32)
    local = wide_ref[pl.ds(0, readers, capacity), :]
    member = wide_ref[pl.ds(1, readers, capacity), :]
    lane = iota((readers, LANES), 1)
    listed = (local >= 0.0) & (lane < entries)
    step = member.astype(jnp.int32) ^ (lax.axis_index("seq") % lanes)
    amount = jnp.sum(listed.astype(jnp.float32), axis=1, keepdims=True).astype(jnp.int32)
    index = jnp.where(listed, step * blocks + local.astype(jnp.int32), 0)
    index_ref[...] = jnp.where(lane == entries, amount, index)
    to_scalars = pltpu.make_async_copy(index_ref, scalar_ref, sems.at[lanes])
    to_scalars.start()
    result = pltpu.make_async_copy(
        attended_ref, out_ref.at[:, pl.ds(room, extra)], out_sems.at[readers]
    )
    result.start()
    to_scalars.wait()
    for copy in copies:
        copy.wait()

    def reader(number, carry):
        chunks = (scalar_ref[number, entries] + (CHUNK_BLOCKS - 1)) // CHUNK_BLOCKS
        groups = jnp.minimum(chunks * (CHUNK_BLOCKS // ROOM_STEP), room // ROOM_STEP)

        def some(group, inner):
            first = group * ROOM_STEP
            tiles = [held_ref[scalar_ref[number, first + i]] for i in range(ROOM_STEP)]
            for i, tile in enumerate(tiles):
                ready_ref[number, first + i] = tile
            return inner

        lax.fori_loop(0, groups, some, carry)
        pltpu.make_async_copy(
            ready_ref.at[number], out_ref.at[number, pl.ds(0, room)], out_sems.at[number]
        ).start()
        return carry

    lax.fori_loop(0, readers, reader, 0)
    result.wait()
    for number in range(readers):
        pltpu.make_async_copy(
            ready_ref.at[number], out_ref.at[number, pl.ds(0, room)], out_sems.at[number]
        ).wait()


def gather_stripes(lanes, steps, room, entries, arrived, attended, pieces):
    blocks, block_tokens, _ = pieces[0].shape
    slots = arrived.shape[0]
    last = arrived.shape[1] // LANES - 1
    readers, extra = attended.shape[:2]
    shape = (readers, room + extra, block_tokens, LANES)
    return pl.pallas_call(
        functools.partial(gather_kernel, lanes, steps, entries),
        out_shape=jax.ShapeDtypeStruct(shape, jnp.bfloat16),
        grid=(1,),
        in_specs=[
            pl.BlockSpec((slots, LANES), lambda _: (0, last)),
            pl.BlockSpec(attended.shape, lambda _: (0,) * 4),
        ]
        + [pl.BlockSpec(memory_space=pl.ANY)] * lanes,
        out_specs=pl.BlockSpec(memory_space=pl.ANY),
        scratch_shapes=[
            pltpu.VMEM((lanes * blocks, block_tokens, LANES), jnp.bfloat16),
            pltpu.VMEM((readers, room, block_tokens, LANES), jnp.bfloat16),
            pltpu.VMEM((slots, LANES), jnp.float32),
            pltpu.VMEM((readers, LANES), jnp.int32),
            pltpu.SMEM((readers, LANES), jnp.int32),
            pltpu.SemaphoreType.DMA((lanes + 1,)),
            pltpu.SemaphoreType.DMA((readers + 1,)),
        ],
        compiler_params=pltpu.CompilerParams(vmem_limit_bytes=VMEM_BYTES),
        cost_estimate=pl.CostEstimate(
            flops=0, bytes_accessed=4 * readers * room * block_tokens * LANES, transcendentals=0
        ),
        name="gather_stripes",
    )(arrived, attended, *pieces)


def vision_kernel(entries, rows_ref, w_ref, out_ref, qkv_ref, blend_ref):
    slots, vit = rows_ref.shape[0], w_ref.shape[0]
    inner = VHEADS * VHD
    qkv_ref[...] = jnp.dot(
        rows_ref[:, :vit], w_ref[...], preferred_element_type=jnp.float32
    ).astype(jnp.bfloat16)
    notes = rows_ref[:, vit:].astype(jnp.float32)
    window_column = jnp.sum(
        jnp.where(iota((slots, LANES), 1) == entries, notes, 0.0), axis=1, keepdims=True
    ).astype(jnp.int32)
    window_row = as_row(window_column)
    itself = iota((slots, slots), 0) == iota((slots, slots), 1)
    allowed = ((window_column == window_row) & (window_row >= 0)) | itself
    blend_ref[...] = jnp.zeros_like(blend_ref)
    for head in range(VHEADS):
        first, last = head * VHD, (head + 1) * VHD
        low, high = first // LANES * LANES, -(-last // LANES) * LANES
        column = low + iota((slots, high - low), 1)
        mine = (column >= first) & (column < last)
        part = lambda offset: qkv_ref[:, offset + low : offset + high]
        keys = jnp.where(mine, part(inner).astype(jnp.float32), 0.0).astype(jnp.bfloat16)
        values = jnp.where(mine, part(2 * inner).astype(jnp.float32), 0.0).astype(jnp.bfloat16)
        scores = lax.dot_general(
            part(0), keys, (((1,), (1,)), ((), ())), preferred_element_type=jnp.float32
        ) * VHD ** (-0.5)
        scores = jnp.where(allowed, scores, HIDDEN)
        weights = jnp.exp(scores - jnp.max(scores, axis=1, keepdims=True))
        total = jnp.sum(weights, axis=1, keepdims=True)
        blended = jnp.dot(weights.astype(jnp.bfloat16), values, preferred_element_type=jnp.float32)
        blend_ref[:, low:high] += blended / total
    devices, tiles, rows, _ = out_ref.shape
    for tile in range(tiles):
        part = blend_ref[:, tile * LANES : (tile + 1) * LANES].astype(jnp.bfloat16)
        out_ref[:, tile] = part.reshape(devices, rows, LANES)


def vision_tiles(devices, entries, arrived, w_qkv):
    slots = arrived.shape[0]
    vit, width = w_qkv.shape
    inner = VHEADS * VHD
    return pl.pallas_call(
        functools.partial(vision_kernel, entries),
        out_shape=jax.ShapeDtypeStruct((devices, inner // LANES, slots // devices, LANES), jnp.bfloat16),
        scratch_shapes=[pltpu.VMEM((slots, width), jnp.bfloat16), pltpu.VMEM((slots, inner), jnp.float32)],
        compiler_params=pltpu.CompilerParams(vmem_limit_bytes=VMEM_BYTES),
        cost_estimate=pl.CostEstimate(
            flops=2 * slots * vit * width + 4 * slots * slots * inner,
            bytes_accessed=2 * vit * width,
            transcendentals=VHEADS * slots * slots,
        ),
        name="vision_tiles",
    )(arrived, w_qkv)


def pick_kernel(target_ref, *refs):
    out_ref = refs[-1]
    returned = jnp.concatenate([ref[...] for ref in refs[:-1]], axis=0)
    rows, slots = target_ref.shape[0], returned.shape[0]
    picked = (target_ref[...] == iota((rows, slots), 1)).astype(jnp.bfloat16)
    out_ref[...] = jnp.dot(picked, returned, preferred_element_type=jnp.float32).astype(jnp.bfloat16)


def pick_rows(target, *returned):
    return pl.pallas_call(
        pick_kernel,
        out_shape=jax.ShapeDtypeStruct((target.shape[0], returned[0].shape[1]), jnp.bfloat16),
        compiler_params=pltpu.CompilerParams(vmem_limit_bytes=VMEM_BYTES),
        name="pick_rows",
    )(target, *returned)


def window_attention(qkv_rows, windows):
    total_rows = qkv_rows.shape[0]
    inner_width = VHEADS * VHD
    query_heads = qkv_rows[:, :inner_width].reshape(total_rows, VHEADS, VHD)
    key_heads = qkv_rows[:, inner_width : 2 * inner_width].reshape(total_rows, VHEADS, VHD)
    value_heads = qkv_rows[:, 2 * inner_width :].reshape(total_rows, VHEADS, VHD)
    is_live = windows >= 0
    every_row = jnp.arange(total_rows)
    scores = jnp.einsum(
        "qhd,khd->hqk", query_heads, key_heads, preferred_element_type=jnp.float32
    ) * VHD ** (-0.5)
    allowed = (windows[:, None] == windows[None, :]) & is_live[None, :] | (
        every_row[:, None] == every_row[None, :]
    )
    scores = jnp.where(allowed[None], scores, -jnp.inf)
    highest = jnp.max(scores, axis=2, keepdims=True)
    weights = jnp.exp(scores - highest)
    totals = jnp.sum(weights, axis=2)
    blended = jnp.einsum(
        "hqk,khd->qhd",
        weights.astype(jnp.bfloat16),
        value_heads,
        preferred_element_type=jnp.float32,
    )
    pieces = (blended / totals.T[:, :, None]).reshape(total_rows, inner_width)
    return pieces.astype(jnp.bfloat16)


def exchange(rows, devices):
    parts = rows.reshape((devices, rows.shape[0] // devices) + rows.shape[1:])
    return lax.all_to_all(parts, "seq", split_axis=0, concat_axis=0, tiled=True).reshape(rows.shape)


def swap(piece, step, devices):
    return lax.ppermute(piece, "seq", [(i, i ^ step) for i in range(devices)])


def vision_rows(arrived, windows, w_qkv):
    vit = w_qkv.shape[0]
    qkv_rows = jnp.dot(arrived[:, :vit], w_qkv, preferred_element_type=jnp.float32).astype(jnp.bfloat16)
    return window_attention(qkv_rows, windows)


def shards(
    patches,
    row_owner,
    window_slot,
    w_patch,
    vit_gain,
    w_qkv,
    queries,
    new_kv,
    kv_cache,
    block_table,
):
    devices = lax.axis_size("seq")
    vit = w_patch.shape[1]
    capacity = 2 * patches.shape[0] // devices
    slots = devices * capacity
    entries = block_table.shape[1]
    per_owner = 2 * entries // devices
    blocks_dev = kv_cache.shape[0]
    lanes = kv_cache.shape[2] // LANES
    striped = devices == 2 * lanes and capacity == kv_cache.shape[1] and entries + 2 <= LANES
    if striped:
        steps = sorted(range(lanes), key=lambda step: (step not in EARLY_STEPS, step < 2, step == 0))
        pieces, block_table = lax.optimization_barrier((stripe(lanes, steps, kv_cache), block_table))
        pieces = [swap(piece, step, devices) if step else piece for step, piece in zip(steps, pieces)]
        early = [steps.index(step) for step in EARLY_STEPS]
    payload, target, request, live = embed_and_route(
        patches, w_patch, vit_gain, row_owner, window_slot, block_table,
        capacity, slots, per_owner, blocks_dev, lanes if striped else None,
    )
    if striped:
        payload, *done = lax.optimization_barrier((payload, *[pieces[place] for place in early]))
        for place, piece in zip(early, done):
            pieces[place] = piece
    arrived = exchange(payload, devices)

    if not striped:
        notes = arrived[:, vit : vit + 2].astype(jnp.int32)
        asked = notes[:, 1].reshape(devices, capacity)[:, :per_owner].reshape(devices * per_owner)
        delivered = exchange(kv_cache[jnp.maximum(asked, 0)], devices)
        attended = vision_rows(arrived, notes[:, 0], w_qkv)
        delivered, attended = lax.optimization_barrier((delivered, attended))
        returned = exchange(attended, devices)
        attention_out = listed_prompt(request, live, queries, new_kv, delivered)
        return (pick_rows(target, returned), attention_out)

    most = jnp.max(arrived[:, vit + entries + 1].astype(jnp.float32))
    attended = vision_tiles(devices, entries, arrived, w_qkv)

    def finish(room):
        def run(arrived, attended, target, live, queries, new_kv, *pieces):
            outgoing = gather_stripes(lanes, steps, room, entries, arrived, attended, pieces)
            delivered = exchange(outgoing.reshape((-1,) + outgoing.shape[2:]), devices).reshape(outgoing.shape)
            attention_out, vision_out = striped_prompt(
                lanes, attended.shape[1], live, queries, new_kv, target, delivered
            )
            return (vision_out, attention_out)

        return run

    rooms = [room for room in (32, 40, 48, 56) if room < entries] + [entries]
    choice = sum((most > room).astype(jnp.int32) for room in rooms[:-1])
    return lax.switch(
        choice, [finish(room) for room in rooms], arrived, attended, target, live, queries, new_kv, *pieces
    )


def solution(mesh):
    in_specs = (
        P(("groups", "seq"), None),
        P(("groups", "seq"), None),
        P(("groups", "seq")),
        P(),
        P(),
        P(),
        P(("groups", "seq"), None),
        P(("groups", "seq"), None),
        P(("groups", "seq"), None, None),
        P(("groups", "seq"), None),
    )
    out_specs = (P(("groups", "seq"), None), P(("groups", "seq"), None))
    return jax.shard_map(shards, mesh=mesh, in_specs=in_specs, out_specs=out_specs, check_vma=False)
```

profile of v0, /device:TPU:1, one launch (start us, length us, event | category | flops | bytes accessed | tf_op | source)
XLA Modules:
  0.0 148.6 jit_solution(8847602535373640350)
XLA Ops:
  0.6 2.6 %stripe.1 = (bf16[64,16,128]{2,1,0:T(8,128)(2,1)}, bf16[64,16,128]{2,1,0:T(8,128)(2,1)}, bf16[64,16,128]{2,1,0:T(8,128)(2,1)}, bf16[64,16,128]{2,1,0:T(8,128)(2,...) custom-call(bf16[64,16,1024]{2,1,0:T(8,128)(2,1)} %cache_ref.1), custom_call_target="tpu_custom_call" | custom-call | tf_op jit(solution)/shard_map/stripe/pallas_call | solution.py:423
  3.3 2.2 %collective-permute-start = (bf16[64,16,128]{2,1,0:T(8,128)(2,1)}, bf16[64,16,128]{2,1,0:T(8,128)(2,1)S(1)}, u32[]{:S(2)}, u32[]{:S(2)}) collective-permute-start(bf16[64,16,128]{2,1,0:T(8,128)(2,1)} %get-tuple-element.257), channel_id=1, source_target_pairs={{0,4},{1,5},{2,6},{3,7},{4,0},{5,1},{6,2},{7,3},{8,12},{9,13},{10,... | collective-permute-start | bytes 786440 | tf_op jit(solution)/shard_map/ppermute | solution.py:634
  5.5 0.6 collective-permute-start.1
  6.1 1.6 %collective-permute-start.2 = (bf16[64,16,128]{2,1,0:T(8,128)(2,1)}, bf16[64,16,128]{2,1,0:T(8,128)(2,1)S(1)}, u32[]{:S(2)}, u32[]{:S(2)}) collective-permute-start(bf16[64,16,128]{2,1,0:T(8,128)(2,1)} %get-tuple-element.259), channel_id=1, source_target_pairs={{0,2},{1,3},{2,0},{3,1},{4,6},{5,7},{6,4},{7,5},{8,10},{9,11},{10,... | collective-permute-start | bytes 786440 | tf_op jit(solution)/shard_map/ppermute | solution.py:634
  7.7 0.3 collective-permute-start.3
  8.1 3.9 %embed_and_route.1 = (bf16[256,1408]{1,0:T(8,128)(2,1)}, s32[128,1]{1,0:T(8,128)S(1)}, s32[1,64]{1,0:T(1,128)}, s32[1,128]{1,0:T(1,128)S(1)}) custom-call(bf16[1176,128]{1,0:T(8,128)(2,1)} %bitcast.13, bf16[1176,1280]{1,0:T(8,128)(2,1)} %w_ref.2, f32[1280]{0:T(1024)} %gain_ref.1, s32[1,128]{1,0:T(1,128)} %bitcast.14, s32[1,128]{1,0:T(1,128)} %bitcast.15, ...), custom_call_target="tpu_custom_call" | custom-call | flops 469237760 | bytes 3966976 | tf_op jit(solution)/shard_map/embed_and_route/pallas_call | solution.py:164
  11.9 0.0 collective-permute-done
  11.9 6.2 %collective-permute-done.1 = bf16[64,16,128]{2,1,0:T(8,128)(2,1)S(1)} collective-permute-done((bf16[64,16,128]{2,1,0:T(8,128)(2,1)}, bf16[64,16,128]{2,1,0:T(8,128)(2,1)S(1)}, u32[]{:S(2)}, u32[]{:S(2)}) %collective-permute-start.1) | collective-permute-done | bytes 262176 | tf_op jit(solution)/shard_map/ppermute | solution.py:634
  18.2 0.0 collective-permute-done.2
  18.2 1.9 %collective-permute-done.3 = bf16[64,16,128]{2,1,0:T(8,128)(2,1)S(1)} collective-permute-done((bf16[64,16,128]{2,1,0:T(8,128)(2,1)}, bf16[64,16,128]{2,1,0:T(8,128)(2,1)S(1)}, u32[]{:S(2)}, u32[]{:S(2)}) %collective-permute-start.3) | collective-permute-done | bytes 262176 | tf_op jit(solution)/shard_map/ppermute | solution.py:634
  20.1 6.9 %all-to-all-start.5 = ((bf16[16,16,1408]{2,1,0:T(8,128)(2,1)}), bf16[16,16,1408]{2,1,0:T(8,128)(2,1)S(1)}, u32[]{:S(2)}, u32[]{:S(2)}) async-start(bf16[16,16,1408]{2,1,0:T(8,128)(2,1)} %bitcast.12), calls=%async_computation.5 | async-start | bytes 1441792 | tf_op jit(solution)/shard_map/all_to_all | solution.py:630
  27.0 2.3 %collective-permute-start.4 = (bf16[64,16,128]{2,1,0:T(8,128)(2,1)}, bf16[64,16,128]{2,1,0:T(8,128)(2,1)S(1)}, u32[]{:S(2)}, u32[]{:S(2)}) collective-permute-start(bf16[64,16,128]{2,1,0:T(8,128)(2,1)} %get-tuple-element.266), channel_id=1, source_target_pairs={{0,6},{1,7},{2,4},{3,5},{4,2},{5,3},{6,0},{7,1},{8,14},{9,15},{10,... | collective-permute-start | bytes 786440 | tf_op jit(solution)/shard_map/ppermute | solution.py:634
  29.3 0.4 collective-permute-start.5
  29.7 0.2 collective-permute-start.6
  29.9 14.8 %all-to-all-done.5 = bf16[16,16,1408]{2,1,0:T(8,128)(2,1)S(1)} async-done(((bf16[16,16,1408]{2,1,0:T(8,128)(2,1)}), bf16[16,16,1408]{2,1,0:T(8,128)(2,1)S(1)}, u32[]{:S(2)}, u32[]{:S(2)}) %all-to-all-start.5) | async-done | bytes 720928 | tf_op jit(solution)/shard_map/all_to_all | solution.py:630
  44.7 0.7 slice_reduce_fusion
  48.0 0.0 copy-start
  48.0 4.9 %vision_tiles.1 = bf16[16,5,16,128]{3,2,1,0:T(8,128)(2,1)S(1)} custom-call(bf16[256,1408]{1,0:T(8,128)(2,1)S(1)} %bitcast.6, bf16[1280,1920]{1,0:T(8,128)(2,1)} %w_ref.3), custom_call_target="tpu_custom_call" | custom-call | flops 1426063360 | bytes 4915200 | tf_op jit(solution)/shard_map/vision_tiles/pallas_call | solution.py:569
  52.9 0.0 collective-permute-done.4
  52.9 0.3 collective-permute-done.5
  53.3 95.4 %conditional.1 = (bf16[128,640]{1,0:T(8,128)(2,1)}, bf16[128,4096]{1,0:T(8,128)(2,1)}) conditional(s32[]{:T(128)} %clamp.3, (bf16[256,1408]{1,0:T(8,128)(2,1)S(1)}, bf16[16,5,16,128]{3,2,1,0:T(8,128)(2,1)S(1)}, bf16[64,16,128]{2,1,0:T(8,128)(2,1)S(1)}, bf16[64,16,128]{2,1,0:T(8,128)(2,1)S(1)}, ...), branch_computations={%region_1.0_spmd, %region_2.0_spmd, %region_3.0_spmd, %region_4.0_... | conditional | flops 2583691264 | bytes 22052880 | solution.py:705
  53.3 3.6 %gather_stripes.6 = bf16[16,45,16,128]{3,2,1,0:T(8,128)(2,1)} custom-call(bf16[256,1408]{1,0:T(8,128)(2,1)S(1)} %get-tuple-element.160.notes_ref, bf16[16,5,16,128]{3,2,1,0:T(8,128)(2,1)S(1)} %get-tuple-element.161.attended_ref, bf16[64,16,128]{2,1,0:T(8,128)(2,1)S(1)} %get-tuple-element.162.refs_0_, bf16[64,16,128]{2,1,0:T(8,128)(2,1)S(1)} %get-tuple-element.163.refs_1_, ...), custom_call_target="tpu_custom_call" | custom-call | bytes 5242880 | tf_op jit(solution)/shard_map/cond/branch_1_fun/gather_stripes/pallas_call | solution.py:502
  56.8 71.9 %all_to_all.26.striped_ref = bf16[16,45,16,128]{3,2,1,0:T(8,128)(2,1)} all-to-all(bf16[16,45,16,128]{3,2,1,0:T(8,128)(2,1)} %gather_stripes.6), channel_id=1, replica_groups=mesh['groups'=2,'seq'=16] {'seq'}, dimensions={0} | all-to-all | bytes 5898240 | tf_op jit(solution)/shard_map/cond/branch_1_fun/all_to_all | solution.py:630
  128.8 19.9 %striped_prompt.6 = (bf16[128,4096]{1,0:T(8,128)(2,1)}, bf16[128,640]{1,0:T(8,128)(2,1)}) custom-call(s32[1,128]{1,0:T(1,128)S(1)} %get-tuple-element.156.live_ref, bf16[128,4096]{1,0:T(8,128)(2,1)S(1)} %get-tuple-element.157.query_ref, bf16[128,1024]{1,0:T(8,128)(2,1)S(1)} %get-tuple-element.158.fresh_ref, s32[128,1]{1,0:T(8,128)S(1)} %get-tuple-element.159.target_ref, ...), custom_call_target="tpu_custom_call" | custom-call | flops 1778384896 | bytes 3833856 | tf_op jit(solution)/shard_map/cond/branch_1_fun/striped_prompt/pallas_call | solution.py:346
  (6 shorter events, 0.0 us)
Async XLA Ops:
  3.3 26.4 %copy-start.2 = (bf16[64,16,128]{2,1,0:T(8,128)(2,1)S(1)}, bf16[64,16,128]{2,1,0:T(8,128)(2,1)}, u32[]{:S(2)}) copy-start(bf16[64,16,128]{2,1,0:T(8,128)(2,1)} %get-tuple-element.268) | copy-start | bytes 786436
  3.3 8.6 %collective-permute-start = (bf16[64,16,128]{2,1,0:T(8,128)(2,1)}, bf16[64,16,128]{2,1,0:T(8,128)(2,1)S(1)}, u32[]{:S(2)}, u32[]{:S(2)}) collective-permute-start(bf16[64,16,128]{2,1,0:T(8,128)(2,1)} %get-tuple-element.257), channel_id=1, source_target_pairs={{0,4},{1,5},{2,6},{3,7},{4,0},{5,1},{6,2},{7,3},{8,12},{9,13},{10,... | collective-permute-start | bytes 786440 | tf_op jit(solution)/shard_map/ppermute | solution.py:634
  5.5 12.7 %collective-permute-start.1 = (bf16[64,16,128]{2,1,0:T(8,128)(2,1)}, bf16[64,16,128]{2,1,0:T(8,128)(2,1)S(1)}, u32[]{:S(2)}, u32[]{:S(2)}) collective-permute-start(bf16[64,16,128]{2,1,0:T(8,128)(2,1)} %get-tuple-element.258), channel_id=1, source_target_pairs={{0,5},{1,4},{2,7},{3,6},{4,1},{5,0},{6,3},{7,2},{8,13},{9,12},{10,... | collective-permute-start | bytes 786440 | tf_op jit(solution)/shard_map/ppermute | solution.py:634
  6.1 12.1 %collective-permute-start.2 = (bf16[64,16,128]{2,1,0:T(8,128)(2,1)}, bf16[64,16,128]{2,1,0:T(8,128)(2,1)S(1)}, u32[]{:S(2)}, u32[]{:S(2)}) collective-permute-start(bf16[64,16,128]{2,1,0:T(8,128)(2,1)} %get-tuple-element.259), channel_id=1, source_target_pairs={{0,2},{1,3},{2,0},{3,1},{4,6},{5,7},{6,4},{7,5},{8,10},{9,11},{10,... | collective-permute-start | bytes 786440 | tf_op jit(solution)/shard_map/ppermute | solution.py:634
  7.7 12.4 %collective-permute-start.3 = (bf16[64,16,128]{2,1,0:T(8,128)(2,1)}, bf16[64,16,128]{2,1,0:T(8,128)(2,1)S(1)}, u32[]{:S(2)}, u32[]{:S(2)}) collective-permute-start(bf16[64,16,128]{2,1,0:T(8,128)(2,1)} %get-tuple-element.260), channel_id=1, source_target_pairs={{0,3},{1,2},{2,1},{3,0},{4,7},{5,6},{6,5},{7,4},{8,11},{9,10},{10,... | collective-permute-start | bytes 786440 | tf_op jit(solution)/shard_map/ppermute | solution.py:634
  20.1 33.1 %copy-start.1 = (bf16[128,1024]{1,0:T(8,128)(2,1)S(1)}, bf16[128,1024]{1,0:T(8,128)(2,1)}, u32[]{:S(2)}) copy-start(bf16[128,1024]{1,0:T(8,128)(2,1)} %param.22) | copy-start | bytes 786436
  20.1 24.6 %all-to-all-start.5 = ((bf16[16,16,1408]{2,1,0:T(8,128)(2,1)}), bf16[16,16,1408]{2,1,0:T(8,128)(2,1)S(1)}, u32[]{:S(2)}, u32[]{:S(2)}) async-start(bf16[16,16,1408]{2,1,0:T(8,128)(2,1)} %bitcast.12), calls=%async_computation.5 | async-start | bytes 1441792 | tf_op jit(solution)/shard_map/all_to_all | solution.py:630
  27.0 25.9 %collective-permute-start.4 = (bf16[64,16,128]{2,1,0:T(8,128)(2,1)}, bf16[64,16,128]{2,1,0:T(8,128)(2,1)S(1)}, u32[]{:S(2)}, u32[]{:S(2)}) collective-permute-start(bf16[64,16,128]{2,1,0:T(8,128)(2,1)} %get-tuple-element.266), channel_id=1, source_target_pairs={{0,6},{1,7},{2,4},{3,5},{4,2},{5,3},{6,0},{7,1},{8,14},{9,15},{10,... | collective-permute-start | bytes 786440 | tf_op jit(solution)/shard_map/ppermute | solution.py:634
  29.3 24.0 %collective-permute-start.5 = (bf16[64,16,128]{2,1,0:T(8,128)(2,1)}, bf16[64,16,128]{2,1,0:T(8,128)(2,1)S(1)}, u32[]{:S(2)}, u32[]{:S(2)}) collective-permute-start(bf16[64,16,128]{2,1,0:T(8,128)(2,1)} %get-tuple-element.267), channel_id=1, source_target_pairs={{0,7},{1,6},{2,5},{3,4},{4,3},{5,2},{6,1},{7,0},{8,15},{9,14},{10,... | collective-permute-start | bytes 786440 | tf_op jit(solution)/shard_map/ppermute | solution.py:634
  29.7 23.6 %collective-permute-start.6 = (bf16[64,16,128]{2,1,0:T(8,128)(2,1)S(1)}, bf16[64,16,128]{2,1,0:T(8,128)(2,1)S(1)}, u32[]{:S(2)}, u32[]{:S(2)}) collective-permute-start(bf16[64,16,128]{2,1,0:T(8,128)(2,1)S(1)} %copy-done.2), channel_id=1, source_target_pairs={{0,1},{1,0},{2,3},{3,2},{4,5},{5,4},{6,7},{7,6},{8,9},{9,8},{10,11... | collective-permute-start | bytes 786440 | tf_op jit(solution)/shard_map/ppermute | solution.py:634
  48.0 5.2 %copy-start = (bf16[128,4096]{1,0:T(8,128)(2,1)S(1)}, bf16[128,4096]{1,0:T(8,128)(2,1)}, u32[]{:S(2)}) copy-start(bf16[128,4096]{1,0:T(8,128)(2,1)} %param.21) | copy-start | bytes 3145732
where the time goes:
time: 149 us
  blocking collectives  71.9 us (48%)
  Pallas kernels  34.8 us (23%)
  waiting for transfers between devices  23.3 us (16%)
  starting transfers between devices  14.6 us (10%)
  between operations  3.29 us (2%)
    all_to_all x1, blocking collectives, exchange(): lax.all_to_all(parts, 'seq', split_axis=0, concat_axis=0, tiled=True)  71.9 us
    pallas_call x1, Pallas kernels, prompt_attention(): pl.pallas_call(kernel, out_shape=tuple((jax.ShapeDtypeStruct(shape, jnp.b...  19.9 us
    all_to_all x1, waiting for transfers between devices, exchange(): lax.all_to_all(parts, 'seq', split_axis=0, concat_axis=0, tiled=True)  14.8 us
    ppermute x7, waiting for transfers between devices, swap(): return lax.ppermute(piece, 'seq', [(i, i ^ step) for i in range(devices)])  8.53 us
    ppermute x7, starting transfers between devices, swap(): return lax.ppermute(piece, 'seq', [(i, i ^ step) for i in range(devices)])  7.71 us
    all_to_all x1, starting transfers between devices, exchange(): lax.all_to_all(parts, 'seq', split_axis=0, concat_axis=0, tiled=True)  6.87 us
    pallas_call x1, Pallas kernels, vision_tiles(): pl.pallas_call(functools.partial(vision_kernel, entries), out_shape=jax.S...  4.86 us
    pallas_call x1, Pallas kernels, embed_and_route(): pl.pallas_call(functools.partial(embed_kernel, capacity, per_owner, block...  3.86 us
  transfers between devices with their start and end apart: 8, of which 4 were waited for; matrix products, arithmetic and copies ran while one was open for 0% of the time, Pallas kernels for 6%

commit v1 on v0

--- a/solution.py
+++ b/solution.py
@@ -19,7 +19,9 @@
 HIDDEN = -1e30
 VMEM_BYTES = 56 * 1024 * 1024
 ROOM_STEP = 8
-EARLY_STEPS = (4, 5, 2, 3)
+SMALL_VMEM_BYTES = 24 * 1024 * 1024
+ROOMS = (28, 32, 36, 40, 48, 64)
+EARLY_STEPS = (4, 2)
 
 
 def iota(shape, axis):
@@ -123,34 +125,33 @@
         notes = jnp.where(lane == 0, windows, jnp.where(lane == 1, asked - 1.0, 0.0))
         notes_ref[...] = notes.astype(jnp.bfloat16)
         return
-    regions = slots // capacity // lanes
+    team = lanes // 2
+    regions = slots // capacity // team
     after = iota((entries, entries), 1) < iota((entries, entries), 0)
-    region_row = jnp.where(live_row, holder_row // lanes, -1)
+    region_row = jnp.where(live_row, holder_row // lanes * 2 + local_row % 2, -1)
     region_column = as_column(region_row)
     region_rank = count((region_column == region_row) & after, 1)
-    local_column, member_column = as_column(local_row), as_column(jnp.where(live_row, holder_row % lanes, 0))
+    local_column = as_column(local_row // 2)
+    member_column = as_column(jnp.where(live_row, holder_row % lanes, 0))
     place = iota((slots, LANES), 0)
-    slot_row, slot_region = place % capacity, place // (capacity * lanes)
+    slot_row, slot_region = place % capacity, place // (capacity * team)
     pad = jnp.zeros((1, LANES - entries), jnp.float32)
     notes = jnp.where(lane == entries, windows, 0.0)
-    most = jnp.zeros((1, 1), jnp.int32)
-    live_ref[...] = jnp.zeros(live_ref.shape, jnp.int32)
     for region in range(regions):
         listed = (region_column == region) & (region_rank == iota((entries, entries), 1))
         pick = lambda column: jnp.sum(
             jnp.where(listed, column, 0).astype(jnp.float32), axis=0, keepdims=True
         )
-        amount = count(region_row == region, 1)
-        most = jnp.maximum(most, amount)
-        live_ref[:, region : region + 1] = amount
         locals_row = jnp.concatenate([pick(local_column + 1) - 1.0, pad], axis=1)
         members_row = jnp.concatenate([pick(member_column), pad], axis=1)
         here = (slot_region == region) & (lane < entries)
         notes = jnp.where(here & (slot_row == 0), locals_row, notes)
         notes = jnp.where(here & (slot_row == 1), members_row, notes)
-    notes = jnp.where(lane == entries + 1, most.astype(jnp.float32), notes)
+        amount = count(region_row == region, 1).astype(jnp.float32)
+        notes = jnp.where((slot_row == 2) & (lane == region), amount, notes)
     notes_ref[...] = notes.astype(jnp.bfloat16)
     request_ref[...] = jnp.zeros(request_ref.shape, jnp.int32)
+    live_ref[...] = jnp.zeros(live_ref.shape, jnp.int32)
 
 
 def embed_and_route(
@@ -307,35 +308,112 @@
     prompt_end(out_ref, sum_ref)
 
 
-def striped_prompt_kernel(
-    lanes, live_ref, query_ref, fresh_ref, target_ref, striped_ref, out_ref, vision_ref, top_ref, sum_ref
-):
-    extra = vision_ref.shape[1] // LANES
-    regions, room, block_tokens = striped_ref.shape[0] // lanes, striped_ref.shape[1] - extra, striped_ref.shape[2]
-    chunk_keys = CHUNK_BLOCKS * block_tokens
-    prompt_begin(query_ref, fresh_ref, top_ref, sum_ref)
-    chunks = [(live_ref[0, region] + (CHUNK_BLOCKS - 1)) // CHUNK_BLOCKS for region in range(regions)]
-
-    def visit(turn, carry):
-        region = (turn >= chunks[0]).astype(jnp.int32)
-        chunk = turn - region * chunks[0]
-        first = jnp.minimum(chunk * CHUNK_BLOCKS, room - CHUNK_BLOCKS)
-        key = iota((1, chunk_keys), 1)
-        shown = (key < (live_ref[0, region] - first) * block_tokens) & (
-            key >= (chunk * CHUNK_BLOCKS - first) * block_tokens
-        )
-        take = lambda lane: striped_ref[region * lanes + lane, pl.ds(first, CHUNK_BLOCKS)].reshape(chunk_keys, HD)
-        prompt_add(query_ref, top_ref, sum_ref, take, shown)
+def striped_prompt_kernel(span_ref, pack_ref, target_ref, striped_ref, *refs):
+    whole_ref, out_refs, (row_ref, sum_ref, top_ref) = None, refs[:-3], refs[-3:]
+    out_ref = out_refs[0]
+    if len(refs) > 4:
+        whole_ref, vision_ref, row_ref, sum_ref, top_ref, out_ref, sem = refs
+    tokens = pack_ref.shape[0]
+    team = striped_ref.shape[1]
+    kv_heads = team // 2
+    heads = out_ref.shape[1] // HD // kv_heads
+    extra = target_ref.shape[1] // LANES
+    room, block_tokens = striped_ref.shape[2] - extra, striped_ref.shape[3]
+    chunk_blocks = CHUNK_BLOCKS // 2
+    half_keys = chunk_blocks * block_tokens
+    causal = iota((tokens, tokens), 1) <= iota((tokens, tokens), 0)
+    causal = jnp.concatenate([causal.astype(jnp.int32)] * heads, axis=0) > 0
+
+    def blend(weights, values):
+        return jnp.dot(weights.astype(jnp.bfloat16), with_ones(values), preferred_element_type=jnp.float32)
+
+    def attend(kv_head, carry):
+        for head in range(heads):
+            row_ref[head * tokens : (head + 1) * tokens, :] = pack_ref[:, head_columns(kv_head * heads + head)]
+        fresh = kv_heads * heads
+        scores = prompt_scores(row_ref[...], pack_ref[:, head_columns(fresh + kv_head)])
+        scores = jnp.where(causal, scores, HIDDEN)
+        top = jnp.max(scores, axis=1, keepdims=True)
+        top_ref[...] = jnp.broadcast_to(top, top_ref.shape)
+        sum_ref[...] = blend(jnp.exp2(scores - top), pack_ref[:, head_columns(fresh + kv_heads + kv_head)])
+
+        chunks = [
+            (jnp.maximum(span_ref[0, 2 * half], span_ref[0, 2 * half + 1]) + (chunk_blocks - 1)) // chunk_blocks
+            for half in range(2)
+        ]
+
+        def visit(turn, inner):
+            half = (turn >= chunks[0]).astype(jnp.int32)
+            done = (turn - half * chunks[0]) * chunk_blocks
+            keys, values, shown = [], [], []
+            for parity in range(2):
+                region = 2 * half + parity
+                amount, base = span_ref[0, region], span_ref[1, region]
+                first = jnp.minimum(base + done, room - chunk_blocks)
+                part = pl.ds(first, chunk_blocks)
+                keys.append(striped_ref[region, kv_head, part].reshape(half_keys, HD))
+                values.append(striped_ref[region, kv_heads + kv_head, part].reshape(half_keys, HD))
+                key = iota((1, half_keys), 1)
+                shown.append(
+                    (
+                        (key < (base + amount - first) * block_tokens)
+                        & (key >= (base + done - first) * block_tokens)
+                    ).astype(jnp.int32)
+                )
+            keys, values = jnp.concatenate(keys, axis=0), jnp.concatenate(values, axis=0)
+            shown = jnp.concatenate(shown, axis=1) > 0
+            scores = jnp.where(shown, prompt_scores(row_ref[...], keys), HIDDEN)
+            old_top = top_ref[...]
+            top = jnp.maximum(old_top, jnp.max(scores, axis=1, keepdims=True))
+            shrink = jnp.exp2(old_top - top)
+            weights = jnp.exp2(scores - jnp.concatenate([top] * (2 * half_keys // HD), axis=1))
+            top_ref[...] = top
+            sum_ref[...] = sum_ref[...] * jnp.concatenate([shrink, shrink], axis=1) + blend(weights, values)
+            return inner
+
+        lax.fori_loop(0, chunks[0] + chunks[1], visit, 0)
+        for head in range(heads):
+            blended = sum_ref[head * tokens : (head + 1) * tokens, :]
+            out_ref[:, head_columns(kv_head * heads + head)] = (
+                blended[:, :HD] / blended[:, HD:]
+            ).astype(jnp.bfloat16)
         return carry
 
-    lax.fori_loop(0, chunks[0] + chunks[1], visit, 0)
-    prompt_end(out_ref, sum_ref)
-    rows, slots = target_ref.shape[0], striped_ref.shape[0] * block_tokens
-    picked = (target_ref[...] == iota((rows, slots), 1)).astype(jnp.bfloat16)
-    for tile in range(extra):
-        vision_ref[:, tile * LANES : (tile + 1) * LANES] = jnp.dot(
-            picked, striped_ref[:, room + tile].reshape(slots, LANES), preferred_element_type=jnp.float32
-        ).astype(jnp.bfloat16)
+    lax.fori_loop(0, kv_heads, attend, 0)
+    if whole_ref is not None:
+        width = out_ref.shape[1]
+        start = pl.multiple_of(lax.axis_index("seq") % 2 * width, width)
+        copy = pltpu.make_async_copy(out_ref, whole_ref.at[:, pl.ds(start, width)], sem)
+        copy.start()
+        regions, team, _, block_tokens, _ = striped_ref.shape
+        slots = regions * team * block_tokens
+        picked = (target_ref[:, :1] == iota((tokens, slots), 1)).astype(jnp.bfloat16)
+        for tile in range(extra):
+            vision_ref[:, tile * LANES : (tile + 1) * LANES] = jnp.dot(
+                picked, striped_ref[:, :, room + tile].reshape(slots, LANES), preferred_element_type=jnp.float32
+            ).astype(jnp.bfloat16)
+        copy.wait()
+
+
+def put_half_kernel(back_ref, whole_ref, out_ref, sem):
+    width = back_ref.shape[1]
+    start = pl.multiple_of((1 - lax.axis_index("seq") % 2) * width, width)
+    copy = pltpu.make_async_copy(back_ref, out_ref.at[:, pl.ds(start, width)], sem)
+    copy.start()
+    copy.wait()
+
+
+def put_half(whole, back):
+    return pl.pallas_call(
+        put_half_kernel,
+        out_shape=jax.ShapeDtypeStruct(whole.shape, whole.dtype),
+        in_specs=[pl.BlockSpec(memory_space=pltpu.VMEM), pl.BlockSpec(memory_space=pl.ANY)],
+        out_specs=pl.BlockSpec(memory_space=pl.ANY),
+        scratch_shapes=[pltpu.SemaphoreType.DMA],
+        input_output_aliases={1: 0},
+        compiler_params=pltpu.CompilerParams(vmem_limit_bytes=SMALL_VMEM_BYTES),
+        name="put_half",
+    )(back, whole)
 
 
 def prompt_attention(kernel, scalars, operands, specs, outs, scratch, keys, name):
@@ -381,19 +459,44 @@
     )[0]
 
 
-def striped_prompt(lanes, extra, live, queries, new_kv, target, striped):
-    keys = striped.shape[1] * striped.shape[2] + queries.shape[0]
-    return prompt_attention(
-        functools.partial(striped_prompt_kernel, lanes), (live,), (queries, new_kv, target, striped),
-        (None,) * 4, [(target.shape[0], extra * LANES)], [], keys, "striped_prompt",
-    )
+def striped_prompt(lanes, extra, span, pack, target, striped, pick):
+    tokens = pack.shape[0]
+    devices, held, block_tokens, _ = striped.shape
+    team = lanes // 2
+    split = striped.reshape(devices // team, team, held, block_tokens, LANES)
+    width = pack.shape[1] - team * HD
+    rows = 2 * width // team // HD * tokens
+    shapes = [(tokens, 2 * width), (tokens, extra * LANES)] if pick else [(tokens, width)]
+    wide_target = jnp.broadcast_to(target, (tokens, extra * LANES))
+    vmem = pl.BlockSpec(memory_space=pltpu.VMEM)
+    return pl.pallas_call(
+        striped_prompt_kernel,
+        out_shape=tuple(jax.ShapeDtypeStruct(shape, jnp.bfloat16) for shape in shapes),
+        in_specs=[pl.BlockSpec(memory_space=pltpu.SMEM), vmem, vmem, vmem],
+        out_specs=(pl.BlockSpec(memory_space=pl.ANY), vmem) if pick else (vmem,),
+        scratch_shapes=[
+            pltpu.VMEM((rows, HD), jnp.bfloat16),
+            pltpu.VMEM((rows, 2 * HD), jnp.float32),
+            pltpu.VMEM((rows, HD), jnp.float32),
+        ]
+        + [pltpu.VMEM((tokens, width), jnp.bfloat16), pltpu.SemaphoreType.DMA] * pick,
+        compiler_params=pltpu.CompilerParams(vmem_limit_bytes=SMALL_VMEM_BYTES),
+        cost_estimate=pl.CostEstimate(
+            flops=4 * tokens * held * block_tokens * width,
+            bytes_accessed=4 * tokens * width + 2 * held * block_tokens * team * HD,
+            transcendentals=tokens * width // HD * held * block_tokens,
+        ),
+        name="striped_prompt_pick" if pick else "striped_prompt",
+    )(span, pack, wide_target, split)
 
 
 def stripe_kernel(lanes, steps, cache_ref, *refs):
     out_refs, held_ref, in_sems, out_sems = refs[:-3], refs[-3], refs[-2], refs[-1]
     member = lax.axis_index("seq") % lanes
+    team = lanes // 2
     chunks = in_sems.shape[0]
-    size = cache_ref.shape[0] // chunks
+    half = cache_ref.shape[0]
+    size = half // chunks
     taken, given = [], []
     for chunk in range(chunks):
         part = pl.ds(chunk * size, size)
@@ -403,22 +506,26 @@
         part = pl.ds(chunk * size, size)
         taken[chunk].wait()
         for place, step in enumerate(steps):
-            column = pl.multiple_of((member ^ step) * LANES, LANES)
-            given.append(
-                pltpu.make_async_copy(
-                    held_ref.at[part, :, pl.ds(column, LANES)],
-                    out_refs[place].at[part],
-                    out_sems.at[chunk, place],
+            lane = member ^ step
+            parity, column = lane // team, lane % team // 2 * KVH + lane % 2
+            for core in range(2):
+                start = pl.multiple_of((column + 2 * core) * LANES, LANES)
+                given.append(
+                    pltpu.make_async_copy(
+                        held_ref.at[part, parity, :, pl.ds(start, LANES)],
+                        out_refs[place].at[pl.ds(core * half + chunk * size, size)],
+                        out_sems.at[chunk, 2 * place + core],
+                    )
                 )
-            )
-            given[-1].start()
+                given[-1].start()
     for copy in given:
         copy.wait()
 
 
 def stripe(lanes, steps, kv_cache):
-    blocks, block_tokens, _ = kv_cache.shape
+    blocks, block_tokens, width = kv_cache.shape
     chunks = 4
+    kv_cache = kv_cache.reshape(blocks // 2, 2, block_tokens, width)
     piece = jax.ShapeDtypeStruct((blocks, block_tokens, LANES), jnp.bfloat16)
     return pl.pallas_call(
         functools.partial(stripe_kernel, lanes, steps),
@@ -428,7 +535,7 @@
         scratch_shapes=[
             pltpu.VMEM(kv_cache.shape, jnp.bfloat16),
             pltpu.SemaphoreType.DMA((chunks,)),
-            pltpu.SemaphoreType.DMA((chunks, len(steps))),
+            pltpu.SemaphoreType.DMA((chunks, 2 * len(steps))),
         ],
         compiler_params=pltpu.CompilerParams(vmem_limit_bytes=VMEM_BYTES),
         name="stripe",
@@ -437,11 +544,15 @@
 
 def gather_kernel(lanes, steps, entries, notes_ref, attended_ref, *refs):
     piece_refs = refs[:lanes]
-    out_ref, held_ref, ready_ref, wide_ref, index_ref, scalar_ref, sems, out_sems = refs[lanes:]
+    out_ref, held_ref, narrow_ref, wide_ref, index_ref, scalar_ref, sems = refs[lanes:]
     blocks = piece_refs[0].shape[0]
     readers, extra = attended_ref.shape[0], attended_ref.shape[1]
     room = out_ref.shape[1] - extra
+    half = blocks // 2
     capacity = notes_ref.shape[0] // readers
+    column = pl.ds(notes_ref.shape[1] - LANES, LANES)
+    noted = pltpu.make_async_copy(notes_ref.at[:, column], narrow_ref, sems.at[lanes + 1])
+    noted.start()
     copies = [
         pltpu.make_async_copy(piece_ref, held_ref.at[pl.ds(step * blocks, blocks)], sems.at[step])
         for step, piece_ref in zip(steps, piece_refs)
@@ -449,7 +560,8 @@
     for copy in copies:
         copy.start()
 
-    wide_ref[...] = notes_ref[...].astype(jnp.float32)
+    noted.wait()
+    wide_ref[...] = narrow_ref[...].astype(jnp.float32)
     local = wide_ref[pl.ds(0, readers, capacity), :]
     member = wide_ref[pl.ds(1, readers, capacity), :]
     lane = iota((readers, LANES), 1)
@@ -457,68 +569,57 @@
     step = member.astype(jnp.int32) ^ (lax.axis_index("seq") % lanes)
     amount = jnp.sum(listed.astype(jnp.float32), axis=1, keepdims=True).astype(jnp.int32)
     index = jnp.where(listed, step * blocks + local.astype(jnp.int32), 0)
+    out_ref[...] = jnp.zeros_like(out_ref)
     index_ref[...] = jnp.where(lane == entries, amount, index)
     to_scalars = pltpu.make_async_copy(index_ref, scalar_ref, sems.at[lanes])
     to_scalars.start()
-    result = pltpu.make_async_copy(
-        attended_ref, out_ref.at[:, pl.ds(room, extra)], out_sems.at[readers]
-    )
-    result.start()
     to_scalars.wait()
     for copy in copies:
         copy.wait()
 
-    def reader(number, carry):
-        chunks = (scalar_ref[number, entries] + (CHUNK_BLOCKS - 1)) // CHUNK_BLOCKS
-        groups = jnp.minimum(chunks * (CHUNK_BLOCKS // ROOM_STEP), room // ROOM_STEP)
-
+    def some_of(reader, chip, base):
         def some(group, inner):
             first = group * ROOM_STEP
-            tiles = [held_ref[scalar_ref[number, first + i]] for i in range(ROOM_STEP)]
-            for i, tile in enumerate(tiles):
-                ready_ref[number, first + i] = tile
+            spots = [scalar_ref[reader, first + i] for i in range(ROOM_STEP)]
+            places = [jnp.minimum(base + first + i, room) for i in range(ROOM_STEP)]
+            for core in range(2):
+                tiles = [held_ref[spot + core * half] for spot in spots]
+                for place, tile in zip(places, tiles):
+                    out_ref[2 * chip + core, place] = tile
             return inner
 
-        lax.fori_loop(0, groups, some, carry)
-        pltpu.make_async_copy(
-            ready_ref.at[number], out_ref.at[number, pl.ds(0, room)], out_sems.at[number]
-        ).start()
-        return carry
-
-    lax.fori_loop(0, readers, reader, 0)
-    result.wait()
-    for number in range(readers):
-        pltpu.make_async_copy(
-            ready_ref.at[number], out_ref.at[number, pl.ds(0, room)], out_sems.at[number]
-        ).wait()
+        return some
+
+    def turn(reader, base):
+        amount = scalar_ref[reader, entries]
+        some = some_of(reader, reader // 2, base)
+        lax.fori_loop(0, (amount + (ROOM_STEP - 1)) // ROOM_STEP, some, 0)
+        return jnp.where(reader % 2 == 0, amount, 0)
+
+    lax.fori_loop(0, readers, turn, 0)
+    out_ref[:, room:] = attended_ref[...]
 
 
 def gather_stripes(lanes, steps, room, entries, arrived, attended, pieces):
     blocks, block_tokens, _ = pieces[0].shape
     slots = arrived.shape[0]
-    last = arrived.shape[1] // LANES - 1
     readers, extra = attended.shape[:2]
     shape = (readers, room + extra, block_tokens, LANES)
     return pl.pallas_call(
         functools.partial(gather_kernel, lanes, steps, entries),
         out_shape=jax.ShapeDtypeStruct(shape, jnp.bfloat16),
-        grid=(1,),
-        in_specs=[
-            pl.BlockSpec((slots, LANES), lambda _: (0, last)),
-            pl.BlockSpec(attended.shape, lambda _: (0,) * 4),
-        ]
+        in_specs=[pl.BlockSpec(memory_space=pl.ANY), pl.BlockSpec(memory_space=pltpu.VMEM)]
         + [pl.BlockSpec(memory_space=pl.ANY)] * lanes,
-        out_specs=pl.BlockSpec(memory_space=pl.ANY),
+        out_specs=pl.BlockSpec(memory_space=pltpu.VMEM),
         scratch_shapes=[
             pltpu.VMEM((lanes * blocks, block_tokens, LANES), jnp.bfloat16),
-            pltpu.VMEM((readers, room, block_tokens, LANES), jnp.bfloat16),
+            pltpu.VMEM((slots, LANES), jnp.bfloat16),
             pltpu.VMEM((slots, LANES), jnp.float32),
             pltpu.VMEM((readers, LANES), jnp.int32),
             pltpu.SMEM((readers, LANES), jnp.int32),
-            pltpu.SemaphoreType.DMA((lanes + 1,)),
-            pltpu.SemaphoreType.DMA((readers + 1,)),
+            pltpu.SemaphoreType.DMA((lanes + 2,)),
         ],
-        compiler_params=pltpu.CompilerParams(vmem_limit_bytes=VMEM_BYTES),
+        compiler_params=pltpu.CompilerParams(vmem_limit_bytes=SMALL_VMEM_BYTES),
         cost_estimate=pl.CostEstimate(
             flops=0, bytes_accessed=4 * readers * room * block_tokens * LANES, transcendentals=0
         ),
@@ -526,13 +627,37 @@
     )(arrived, attended, *pieces)
 
 
-def vision_kernel(entries, rows_ref, w_ref, out_ref, qkv_ref, blend_ref):
+def vision_kernel(
+    entries, rooms, rows_ref, w_hbm_ref, out_ref, own_ref, other_ref, choice_ref, w_ref, qkv_ref, blend_ref, wide_ref, sems
+):
     slots, vit = rows_ref.shape[0], w_ref.shape[0]
     inner = VHEADS * VHD
-    qkv_ref[...] = jnp.dot(
-        rows_ref[:, :vit], w_ref[...], preferred_element_type=jnp.float32
-    ).astype(jnp.bfloat16)
+    copies = []
+    for third in range(3):
+        part = pl.ds(third * inner, inner)
+        copies.append(pltpu.make_async_copy(w_hbm_ref.at[:, part], w_ref.at[:, part], sems.at[third]))
+        copies[-1].start()
     notes = rows_ref[:, vit:].astype(jnp.float32)
+    wide_ref[...] = notes
+    device = lax.axis_index("seq")
+    capacity = slots // out_ref.shape[0]
+    first_row = (device - device % 2) * capacity + 2
+    amounts = [wide_ref[pl.ds(first_row + i * capacity, 1), :].astype(jnp.int32) for i in range(2)]
+    second = device % 2 > 0
+    nothing = jnp.zeros_like(amounts[0])
+    own_ref[...] = jnp.concatenate(
+        [jnp.where(second, amounts[1], amounts[0]), jnp.where(second, amounts[0], nothing)], axis=0
+    )
+    other_ref[...] = jnp.concatenate(
+        [jnp.where(second, amounts[0], amounts[1]), jnp.where(second, nothing, amounts[0])], axis=0
+    )
+    chips = out_ref.shape[0] // 2
+    pooled = wide_ref[pl.ds(2, chips, 2 * capacity), :] + wide_ref[pl.ds(2 + capacity, chips, 2 * capacity), :]
+    needed = jnp.max(jnp.where(iota((chips, LANES), 1) < entries, pooled, 0.0)).astype(jnp.int32)
+    choice = 0
+    for room in rooms:
+        choice = choice + jnp.where(needed > room, 1, 0)
+    choice_ref[0, 0] = choice
     window_column = jnp.sum(
         jnp.where(iota((slots, LANES), 1) == entries, notes, 0.0), axis=1, keepdims=True
     ).astype(jnp.int32)
@@ -540,6 +665,12 @@
     itself = iota((slots, slots), 0) == iota((slots, slots), 1)
     allowed = ((window_column == window_row) & (window_row >= 0)) | itself
     blend_ref[...] = jnp.zeros_like(blend_ref)
+    for third, copy in enumerate(copies):
+        part = slice(third * inner, (third + 1) * inner)
+        copy.wait()
+        qkv_ref[:, part] = jnp.dot(
+            rows_ref[:, :vit], w_ref[:, part], preferred_element_type=jnp.float32
+        ).astype(jnp.bfloat16)
     for head in range(VHEADS):
         first, last = head * VHD, (head + 1) * VHD
         low, high = first // LANES * LANES, -(-last // LANES) * LANES
@@ -562,14 +693,27 @@
         out_ref[:, tile] = part.reshape(devices, rows, LANES)
 
 
-def vision_tiles(devices, entries, arrived, w_qkv):
+def vision_tiles(devices, entries, rooms, arrived, w_qkv):
     slots = arrived.shape[0]
     vit, width = w_qkv.shape
     inner = VHEADS * VHD
     return pl.pallas_call(
-        functools.partial(vision_kernel, entries),
-        out_shape=jax.ShapeDtypeStruct((devices, inner // LANES, slots // devices, LANES), jnp.bfloat16),
-        scratch_shapes=[pltpu.VMEM((slots, width), jnp.bfloat16), pltpu.VMEM((slots, inner), jnp.float32)],
+        functools.partial(vision_kernel, entries, rooms),
+        out_shape=(
+            jax.ShapeDtypeStruct((devices, inner // LANES, slots // devices, LANES), jnp.bfloat16),
+            jax.ShapeDtypeStruct((2, LANES), jnp.int32),
+            jax.ShapeDtypeStruct((2, LANES), jnp.int32),
+            jax.ShapeDtypeStruct((1, 1), jnp.int32),
+        ),
+        in_specs=[pl.BlockSpec(memory_space=pltpu.VMEM), pl.BlockSpec(memory_space=pl.ANY)],
+        out_specs=(pl.BlockSpec(memory_space=pltpu.VMEM),) * 3 + (pl.BlockSpec(memory_space=pltpu.SMEM),),
+        scratch_shapes=[
+            pltpu.VMEM((vit, width), jnp.bfloat16),
+            pltpu.VMEM((slots, width), jnp.bfloat16),
+            pltpu.VMEM((slots, inner), jnp.float32),
+            pltpu.VMEM((slots, LANES), jnp.float32),
+            pltpu.SemaphoreType.DMA((3,)),
+        ],
         compiler_params=pltpu.CompilerParams(vmem_limit_bytes=VMEM_BYTES),
         cost_estimate=pl.CostEstimate(
             flops=2 * slots * vit * width + 4 * slots * slots * inner,
@@ -628,6 +772,23 @@
 def exchange(rows, devices):
     parts = rows.reshape((devices, rows.shape[0] // devices) + rows.shape[1:])
     return lax.all_to_all(parts, "seq", split_axis=0, concat_axis=0, tiled=True).reshape(rows.shape)
+
+
+def core_index():
+    return lax.axis_index("seq") % 2
+
+
+def head_half(queries, new_kv, core):
+    width, kv_width = queries.shape[1] // 2, new_kv.shape[1] // 4
+    part = lambda array, start, size: lax.dynamic_slice_in_dim(array, start, size, 1)
+    return jnp.concatenate(
+        [
+            part(queries, core * width, width),
+            part(new_kv, core * kv_width, kv_width),
+            part(new_kv, 2 * kv_width + core * kv_width, kv_width),
+        ],
+        axis=1,
+    )
 
 
 def swap(piece, step, devices):
@@ -686,24 +847,26 @@
         attention_out = listed_prompt(request, live, queries, new_kv, delivered)
         return (pick_rows(target, returned), attention_out)
 
-    most = jnp.max(arrived[:, vit + entries + 1].astype(jnp.float32))
-    attended = vision_tiles(devices, entries, arrived, w_qkv)
+    rooms = [room for room in ROOMS if room < 2 * entries] + [2 * entries]
+    attended, own_span, other_span, choice = vision_tiles(devices, entries, rooms[:-1], arrived, w_qkv)
 
     def finish(room):
-        def run(arrived, attended, target, live, queries, new_kv, *pieces):
+        def run(arrived, attended, target, own_span, other_span, queries, new_kv, *pieces):
             outgoing = gather_stripes(lanes, steps, room, entries, arrived, attended, pieces)
             delivered = exchange(outgoing.reshape((-1,) + outgoing.shape[2:]), devices).reshape(outgoing.shape)
-            attention_out, vision_out = striped_prompt(
-                lanes, attended.shape[1], live, queries, new_kv, target, delivered
-            )
-            return (vision_out, attention_out)
+            extra = attended.shape[1]
+            own_pack, other_pack = [head_half(queries, new_kv, core) for core in (core_index(), 1 - core_index())]
+            other_pack = swap(other_pack, 1, devices)
+            (other_out,) = striped_prompt(lanes, extra, other_span, other_pack, target, delivered, False)
+            back = swap(other_out, 1, devices)
+            own_out, vision_out = striped_prompt(lanes, extra, own_span, own_pack, target, delivered, True)
+            return (vision_out, put_half(own_out, back))
 
         return run
 
-    rooms = [room for room in (32, 40, 48, 56) if room < entries] + [entries]
-    choice = sum((most > room).astype(jnp.int32) for room in rooms[:-1])
     return lax.switch(
-        choice, [finish(room) for room in rooms], arrived, attended, target, live, queries, new_kv, *pieces
+        choice[0, 0], [finish(room) for room in rooms],
+        arrived, attended, target, own_span, other_span, queries, new_kv, *pieces,
     )
 
 

time: 149 us -> 135 us (0.906)
  the two profiles are of different devices: /device:TPU:1 before, /device:TPU:13 now
where the time goes in v1:
time: 135 us; the launch traced here: 136 us
  waiting for transfers between devices  80.8 us (60%)
  Pallas kernels  29.5 us (22%)
  starting transfers between devices  18.3 us (14%)
  local copies, waits for them, and re-layouts  4.8 us (4%)
    all_to_all x2, waiting for transfers between devices, exchange(): lax.all_to_all(parts, 'seq', split_axis=0, concat_axis=0, tiled=True)  69.2 us
    pallas_call x2, Pallas kernels, striped_prompt(): pl.pallas_call(striped_prompt_kernel, out_shape=tuple((jax.ShapeDtypeStru...  15.2 us
    all_to_all x2, starting transfers between devices, exchange(): lax.all_to_all(parts, 'seq', split_axis=0, concat_axis=0, tiled=True)  13.7 us
    ppermute x9, waiting for transfers between devices, swap(): return lax.ppermute(piece, 'seq', [(i, i ^ step) for i in range(devices)])  11.7 us
    ppermute x9, starting transfers between devices, swap(): return lax.ppermute(piece, 'seq', [(i, i ^ step) for i in range(devices)])  4.65 us
    pallas_call x1, Pallas kernels, vision_tiles(): pl.pallas_call(functools.partial(vision_kernel, entries, rooms), out_shap...  4.39 us
    pallas_call x1, Pallas kernels, embed_and_route(): pl.pallas_call(functools.partial(embed_kernel, capacity, per_owner, block...  3.93 us
    pallas_call x1, Pallas kernels, gather_stripes(): pl.pallas_call(functools.partial(gather_kernel, lanes, steps, entries), o...  2.93 us
  transfers between devices with their start and end apart: 11, of which 6 were waited for; matrix products, arithmetic and copies ran while one was open for 2% of the time, Pallas kernels for 12%

profile of v1, /device:TPU:13, one launch (start us, length us, event | category | flops | bytes accessed | tf_op | source)
XLA Modules:
  0.0 135.8 jit_solution(3556250006045957960)
XLA Ops:
  0.6 2.9 %stripe.1 = (bf16[64,16,128]{2,1,0:T(8,128)(2,1)}, bf16[64,16,128]{2,1,0:T(8,128)(2,1)}, bf16[64,16,128]{2,1,0:T(8,128)(2,1)}, bf16[64,16,128]{2,1,0:T(8,128)(2,...) custom-call(bf16[32,2,16,1024]{3,2,1,0:T(8,128)(2,1)} %bitcast.39), custom_call_target="tpu_custom_call" | custom-call | tf_op jit(solution)/shard_map/stripe/pallas_call | solution.py:530
  3.9 3.9 %embed_and_route.1 = (bf16[256,1408]{1,0:T(8,128)(2,1)}, s32[128,1]{1,0:T(8,128)}, s32[1,64]{1,0:T(1,128)}, s32[1,128]{1,0:T(1,128)}) custom-call(bf16[1176,128]{1,0:T(8,128)(2,1)} %bitcast.41, bf16[1176,1280]{1,0:T(8,128)(2,1)} %w_ref.1, f32[1280]{0:T(1024)} %gain_ref.1, s32[1,128]{1,0:T(1,128)} %bitcast.49, s32[1,128]{1,0:T(1,128)} %bitcast.50, ...), custom_call_target="tpu_custom_call" | custom-call | flops 469237760 | bytes 3966976 | tf_op jit(solution)/shard_map/embed_and_route/pallas_call | solution.py:165
  7.9 3.1 %collective-permute-done.14 = bf16[64,16,128]{2,1,0:T(8,128)(2,1)S(1)} collective-permute-done((bf16[64,16,128]{2,1,0:T(8,128)(2,1)}, bf16[64,16,128]{2,1,0:T(8,128)(2,1)S(1)}, u32[]{:S(2)}, u32[]{:S(2)}) %collective-permute-start.14) | collective-permute-done | bytes 262176 | tf_op jit(solution)/shard_map/ppermute | solution.py:795
  11.0 7.7 %all-to-all-start.7 = ((bf16[16,16,1408]{2,1,0:T(8,128)(2,1)}), bf16[16,16,1408]{2,1,0:T(8,128)(2,1)S(1)}, u32[]{:S(2)}, u32[]{:S(2)}) async-start(bf16[16,16,1408]{2,1,0:T(8,128)(2,1)} %bitcast.40), calls=%async_computation.7 | async-start | bytes 1441792 | tf_op jit(solution)/shard_map/all_to_all | solution.py:774
  18.7 0.5 collective-permute-start.16
  19.4 2.3 %collective-permute-start.18 = (bf16[64,16,128]{2,1,0:T(8,128)(2,1)}, bf16[64,16,128]{2,1,0:T(8,128)(2,1)S(1)}, u32[]{:S(2)}, u32[]{:S(2)}) collective-permute-start(bf16[64,16,128]{2,1,0:T(8,128)(2,1)} %get-tuple-element.377), channel_id=1, source_target_pairs={{0,6},{1,7},{2,4},{3,5},{4,2},{5,3},{6,0},{7,1},{8,14},{9,15},{10,... | collective-permute-start | bytes 786440 | tf_op jit(solution)/shard_map/ppermute | solution.py:795
  21.7 0.4 collective-permute-start.19
  22.1 0.3 collective-permute-start.20
  22.4 14.5 %all-to-all-done.7 = bf16[16,16,1408]{2,1,0:T(8,128)(2,1)S(1)} async-done(((bf16[16,16,1408]{2,1,0:T(8,128)(2,1)}), bf16[16,16,1408]{2,1,0:T(8,128)(2,1)S(1)}, u32[]{:S(2)}, u32[]{:S(2)}) %all-to-all-start.7) | async-done | bytes 720928 | tf_op jit(solution)/shard_map/all_to_all | solution.py:774
  36.9 4.4 %vision_tiles.1 = (bf16[16,5,16,128]{3,2,1,0:T(8,128)(2,1)S(1)}, s32[2,128]{1,0:T(2,128)S(1)}, s32[2,128]{1,0:T(2,128)S(1)}, s32[1,1]{1,0:T(1,128)}) custom-call(bf16[256,1408]{1,0:T(8,128)(2,1)S(1)} %bitcast.31, bf16[1280,1920]{1,0:T(8,128)(2,1)} %w_hbm_ref.1), custom_call_target="tpu_custom_call" | custom-call | flops 1426063360 | bytes 4915200 | tf_op jit(solution)/shard_map/vision_tiles/pallas_call | solution.py:700
  42.0 1.0 collective-permute-done.18
  43.0 5.6 %collective-permute-done.19 = bf16[64,16,128]{2,1,0:T(8,128)(2,1)S(1)} collective-permute-done((bf16[64,16,128]{2,1,0:T(8,128)(2,1)S(1)}, bf16[64,16,128]{2,1,0:T(8,128)(2,1)S(1)}, u32[]{:S(2)}, u32[]{:S(2)}) %collective-permute-start.19) | collective-permute-done | bytes 262176 | tf_op jit(solution)/shard_map/ppermute | solution.py:795
  48.6 87.2 %conditional.1 = (bf16[128,640]{1,0:T(8,128)(2,1)}, bf16[128,4096]{1,0:T(8,128)(2,1)}) conditional(s32[]{:T(128)} %bitcast.20, (bf16[128,4096]{1,0:T(8,128)(2,1)}, bf16[128,1024]{1,0:T(8,128)(2,1)}, s32[128,1]{1,0:T(8,128)}, bf16[256,1408]{1,0:T(8,128)(2,1)S(1)}, bf16[16,5,16,128]{3,2,1,0:T(8,128)(2,1)S(1)}, ...), branch_computations={%region_0.1_spmd, %region_1.2_spmd, %region_2.3_spmd, %region_3.4_... | conditional | flops 4466671616 | bytes 103977160 | solution.py:867
  48.6 2.9 %gather_stripes.9 = bf16[16,41,16,128]{3,2,1,0:T(8,128)(2,1)S(1)} custom-call(bf16[256,1408]{1,0:T(8,128)(2,1)S(1)} %get-tuple-element.248.notes_ref, bf16[16,5,16,128]{3,2,1,0:T(8,128)(2,1)S(1)} %get-tuple-element.249.attended_ref, bf16[64,16,128]{2,1,0:T(8,128)(2,1)S(1)} %get-tuple-element.250.refs_0_, ...), custom_call_target="tpu_custom_call" | custom-call | bytes 4718592 | tf_op jit(solution)/shard_map/cond/branch_2_fun/gather_stripes/pallas_call | solution.py:608
  51.5 1.5 %copy-done.4 = bf16[16,41,16,128]{3,2,1,0:T(8,128)(2,1)} copy-done((bf16[16,41,16,128]{3,2,1,0:T(8,128)(2,1)}, bf16[16,41,16,128]{3,2,1,0:T(8,128)(2,1)S(1)}, u32[]{:S(2)}) %copy-start.4) | copy-done | bytes 2687000 | tf_op jit(solution)/shard_map/cond
  53.0 6.0 %all-to-all-start.2 = ((bf16[16,41,16,128]{3,2,1,0:T(8,128)(2,1)}), bf16[16,41,16,128]{3,2,1,0:T(8,128)(2,1)S(1)}, u32[]{:S(2)}, u32[]{:S(2)}) async-start(bf16[16,41,16,128]{3,2,1,0:T(8,128)(2,1)} %copy-done.4), calls=%async_computation.2 | async-start | bytes 5373952 | tf_op jit(solution)/shard_map/cond/branch_2_fun/all_to_all | solution.py:774
  59.1 2.1 %constant_dynamic-slice_fusion.14 = (bf16[128,2048]{1,0:T(8,128)(2,1)S(1)}, bf16[128,2048]{1,0:T(8,128)(2,1)}) fusion(bf16[128,4096]{1,0:T(8,128)(2,1)} %get-tuple-element.245, s32[]{:T(128)S(6)} %select_n.140, s32[]{:T(128)S(6)} %select_n.137), kind=kLoop, calls=%fused_computation.20 | loop fusion | bytes 2097160 | tf_op jit(solution)/shard_map/cond/branch_2_fun/dynamic_slice | solution.py:783
  61.2 0.9 pad_maximum_fusion.5
  62.1 0.4 collective-permute-start.4
  62.5 1.9 %collective-permute-done.4.pack_ref = bf16[128,2560]{1,0:T(8,128)(2,1)S(1)} collective-permute-done((bf16[128,2560]{1,0:T(8,128)(2,1)}, bf16[128,2560]{1,0:T(8,128)(2,1)S(1)}, u32[]{:S(2)}, u32[]{:S(2)}) %collective-permute-start.4) | collective-permute-done | bytes 655392 | tf_op jit(solution)/shard_map/cond/branch_2_fun/ppermute | solution.py:795
  64.4 54.7 %all-to-all-done.2 = bf16[16,41,16,128]{3,2,1,0:T(8,128)(2,1)S(1)} async-done(((bf16[16,41,16,128]{3,2,1,0:T(8,128)(2,1)}), bf16[16,41,16,128]{3,2,1,0:T(8,128)(2,1)S(1)}, u32[]{:S(2)}, u32[]{:S(2)}) %all-to-all-start.2) | async-done | bytes 2687008 | tf_op jit(solution)/shard_map/cond/branch_2_fun/all_to_all | solution.py:774
  119.2 7.1 %striped_prompt.9 = bf16[128,2048]{1,0:T(8,128)(2,1)S(1)} custom-call(s32[2,128]{1,0:T(2,128)S(1)} %get-tuple-element.259.span_ref, bf16[128,2560]{1,0:T(8,128)(2,1)S(1)} %collective-permute-done.4.pack_ref, s32[128,640]{1,0:T(8,128)S(1)} %broadcast_in_dim.37.target_ref, bf16[4,4,41,16,128]{4,3,2,1,0:T(8,128)(2,1)S(1)} %bitcast.25), custom_call_target="tpu_custom_call" | custom-call | flops 687865856 | bytes 1720320 | tf_op jit(solution)/shard_map/cond/branch_2_fun/striped_prompt/pallas_call | solution.py:472
  126.6 8.1 %striped_prompt_pick.9 = (bf16[128,4096]{1,0:T(8,128)(2,1)S(1)}, bf16[128,640]{1,0:T(8,128)(2,1)}) custom-call(s32[2,128]{1,0:T(2,128)S(1)} %get-tuple-element.244.span_ref, bf16[128,2560]{1,0:T(8,128)(2,1)S(1)} %pad_maximum_fusion.4.pack_ref, s32[128,640]{1,0:T(8,128)S(1)} %broadcast_in_dim.37.target_ref, bf16[4,4,41,16,128]{4,3,2,1,0:T(8,128)(2,1)S(1)} %bitcast.26), custom_call_target="tpu_custom_call" | custom-call | flops 687865856 | bytes 1720320 | tf_op jit(solution)/shard_map/cond/branch_2_fun/striped_prompt_pick/pallas_call | solution.py:472
  134.9 1.0 copy-done.9
  (26 shorter events, 1.1 us)
Async XLA Ops:
  3.6 7.5 %collective-permute-start.14 = (bf16[64,16,128]{2,1,0:T(8,128)(2,1)}, bf16[64,16,128]{2,1,0:T(8,128)(2,1)S(1)}, u32[]{:S(2)}, u32[]{:S(2)}) collective-permute-start(bf16[64,16,128]{2,1,0:T(8,128)(2,1)} %get-tuple-element.367), channel_id=1, source_target_pairs={{0,4},{1,5},{2,6},{3,7},{4,0},{5,1},{6,2},{7,3},{8,12},{9,13},{10,... | collective-permute-start | bytes 786440 | tf_op jit(solution)/shard_map/ppermute | solution.py:795
  3.8 7.2 %collective-permute-start.15 = (bf16[64,16,128]{2,1,0:T(8,128)(2,1)}, bf16[64,16,128]{2,1,0:T(8,128)(2,1)S(1)}, u32[]{:S(2)}, u32[]{:S(2)}) collective-permute-start(bf16[64,16,128]{2,1,0:T(8,128)(2,1)} %get-tuple-element.368), channel_id=1, source_target_pairs={{0,2},{1,3},{2,0},{3,1},{4,6},{5,7},{6,4},{7,5},{8,10},{9,11},{10,... | collective-permute-start | bytes 786440 | tf_op jit(solution)/shard_map/ppermute | solution.py:795
  7.9 13.8 %copy-start.42 = (bf16[64,16,128]{2,1,0:T(8,128)(2,1)S(1)}, bf16[64,16,128]{2,1,0:T(8,128)(2,1)}, u32[]{:S(2)}) copy-start(bf16[64,16,128]{2,1,0:T(8,128)(2,1)} %get-tuple-element.378) | copy-start | bytes 786436
  7.9 14.2 %copy-start.41 = (bf16[64,16,128]{2,1,0:T(8,128)(2,1)S(1)}, bf16[64,16,128]{2,1,0:T(8,128)(2,1)}, u32[]{:S(2)}) copy-start(bf16[64,16,128]{2,1,0:T(8,128)(2,1)} %get-tuple-element.379) | copy-start | bytes 786436
  11.0 25.9 %all-to-all-start.7 = ((bf16[16,16,1408]{2,1,0:T(8,128)(2,1)}), bf16[16,16,1408]{2,1,0:T(8,128)(2,1)S(1)}, u32[]{:S(2)}, u32[]{:S(2)}) async-start(bf16[16,16,1408]{2,1,0:T(8,128)(2,1)} %bitcast.40), calls=%async_computation.7 | async-start | bytes 1441792 | tf_op jit(solution)/shard_map/all_to_all | solution.py:774
  18.7 23.2 %collective-permute-start.16 = (bf16[64,16,128]{2,1,0:T(8,128)(2,1)}, bf16[64,16,128]{2,1,0:T(8,128)(2,1)S(1)}, u32[]{:S(2)}, u32[]{:S(2)}) collective-permute-start(bf16[64,16,128]{2,1,0:T(8,128)(2,1)} %get-tuple-element.375), channel_id=1, source_target_pairs={{0,3},{1,2},{2,1},{3,0},{4,7},{5,6},{6,5},{7,4},{8,11},{9,10},{10,... | collective-permute-start | bytes 786440 | tf_op jit(solution)/shard_map/ppermute | solution.py:795
  19.3 22.7 %collective-permute-start.17 = (bf16[64,16,128]{2,1,0:T(8,128)(2,1)}, bf16[64,16,128]{2,1,0:T(8,128)(2,1)S(1)}, u32[]{:S(2)}, u32[]{:S(2)}) collective-permute-start(bf16[64,16,128]{2,1,0:T(8,128)(2,1)} %get-tuple-element.376), channel_id=1, source_target_pairs={{0,5},{1,4},{2,7},{3,6},{4,1},{5,0},{6,3},{7,2},{8,13},{9,12},{10,... | collective-permute-start | bytes 786440 | tf_op jit(solution)/shard_map/ppermute | solution.py:795
  19.4 23.6 %collective-permute-start.18 = (bf16[64,16,128]{2,1,0:T(8,128)(2,1)}, bf16[64,16,128]{2,1,0:T(8,128)(2,1)S(1)}, u32[]{:S(2)}, u32[]{:S(2)}) collective-permute-start(bf16[64,16,128]{2,1,0:T(8,128)(2,1)} %get-tuple-element.377), channel_id=1, source_target_pairs={{0,6},{1,7},{2,4},{3,5},{4,2},{5,3},{6,0},{7,1},{8,14},{9,15},{10,... | collective-permute-start | bytes 786440 | tf_op jit(solution)/shard_map/ppermute | solution.py:795
  21.7 26.9 %collective-permute-start.19 = (bf16[64,16,128]{2,1,0:T(8,128)(2,1)S(1)}, bf16[64,16,128]{2,1,0:T(8,128)(2,1)S(1)}, u32[]{:S(2)}, u32[]{:S(2)}) collective-permute-start(bf16[64,16,128]{2,1,0:T(8,128)(2,1)S(1)} %copy-done.42), channel_id=1, source_target_pairs={{0,7},{1,6},{2,5},{3,4},{4,3},{5,2},{6,1},{7,0},{8,15},{9,14},{10,... | collective-permute-start | bytes 786440 | tf_op jit(solution)/shard_map/ppermute | solution.py:795
  22.1 26.5 %collective-permute-start.20 = (bf16[64,16,128]{2,1,0:T(8,128)(2,1)S(1)}, bf16[64,16,128]{2,1,0:T(8,128)(2,1)S(1)}, u32[]{:S(2)}, u32[]{:S(2)}) collective-permute-start(bf16[64,16,128]{2,1,0:T(8,128)(2,1)S(1)} %copy-done.41), channel_id=1, source_target_pairs={{0,1},{1,0},{2,3},{3,2},{4,5},{5,4},{6,7},{7,6},{8,9},{9,8},{10,11... | collective-permute-start | bytes 786440 | tf_op jit(solution)/shard_map/ppermute | solution.py:795
  51.5 1.5 %copy-start.4 = (bf16[16,41,16,128]{3,2,1,0:T(8,128)(2,1)}, bf16[16,41,16,128]{3,2,1,0:T(8,128)(2,1)S(1)}, u32[]{:S(2)}) copy-start(bf16[16,41,16,128]{3,2,1,0:T(8,128)(2,1)S(1)} %gather_stripes.9) | copy-start | bytes 8060932 | tf_op jit(solution)/shard_map/cond
  53.0 6.0 %copy-start.19 = (bf16[128,1024]{1,0:T(8,128)(2,1)S(1)}, bf16[128,1024]{1,0:T(8,128)(2,1)}, u32[]{:S(2)}) copy-start(bf16[128,1024]{1,0:T(8,128)(2,1)} %get-tuple-element.246) | copy-start | bytes 786436 | tf_op jit(solution)/shard_map/cond
  53.0 66.0 %all-to-all-start.2 = ((bf16[16,41,16,128]{3,2,1,0:T(8,128)(2,1)}), bf16[16,41,16,128]{3,2,1,0:T(8,128)(2,1)S(1)}, u32[]{:S(2)}, u32[]{:S(2)}) async-start(bf16[16,41,16,128]{3,2,1,0:T(8,128)(2,1)} %copy-done.4), calls=%async_computation.2 | async-start | bytes 5373952 | tf_op jit(solution)/shard_map/cond/branch_2_fun/all_to_all | solution.py:774
  59.1 3.4 %copy-start.25 = (s32[128,1]{1,0:T(8,128)S(1)}, s32[128,1]{1,0:T(8,128)}, u32[]{:S(2)}) copy-start(s32[128,1]{1,0:T(8,128)} %get-tuple-element.416) | copy-start | bytes 1540 | tf_op jit(solution)/shard_map/cond
  62.1 2.3 %collective-permute-start.4 = (bf16[128,2560]{1,0:T(8,128)(2,1)}, bf16[128,2560]{1,0:T(8,128)(2,1)S(1)}, u32[]{:S(2)}, u32[]{:S(2)}) collective-permute-start(bf16[128,2560]{1,0:T(8,128)(2,1)} %pad_maximum_fusion.5), channel_id=1, source_target_pairs={{0,1},{1,0},{2,3},{3,2},{4,5},{5,4},{6,7},{7,6},{8,9},{9,8},{10,11... | collective-permute-start | bytes 1966088 | tf_op jit(solution)/shard_map/cond/branch_2_fun/ppermute | solution.py:795
  119.2 7.4 %copy-start.32 = (bf16[128,2048]{1,0:T(8,128)(2,1)S(1)}, bf16[128,2048]{1,0:T(8,128)(2,1)}, u32[]{:S(2)}) copy-start(bf16[128,2048]{1,0:T(8,128)(2,1)} %get-tuple-element.502) | copy-start | bytes 1572868 | tf_op jit(solution)/shard_map/cond
  126.3 8.5 %collective-permute-start.5 = (bf16[128,2048]{1,0:T(8,128)(2,1)S(1)}, bf16[128,2048]{1,0:T(8,128)(2,1)S(1)}, u32[]{:S(2)}, u32[]{:S(2)}) collective-permute-start(bf16[128,2048]{1,0:T(8,128)(2,1)S(1)} %striped_prompt.9), channel_id=1, source_target_pairs={{0,1},{1,0},{2,3},{3,2},{4,5},{5,4},{6,7},{7,6},{8,9},{9,8},{10,11... | collective-permute-start | bytes 1572872 | tf_op jit(solution)/shard_map/cond/branch_2_fun/ppermute | solution.py:795
  134.8 1.0 copy-start.9
